TPU v7x, 32 devices: a whole 2x2x4 slice. The times are simulated.
32 devices in a mesh: gx: 8 (over z, y), gy: 4 (over x, core).
Axes of the slice: x: 2, y: 2, z: 4, core: 2. Of those that a mesh axis runs over, the one named last changes fastest.
Arguments:
- initial_warmth_field: float32 [16, 1024, 512], P(None, 'gx', 'gy'), may hold values from -8 to 8
- horizontal_motion_pair: float32 [2, 16, 1024, 512], P(None, None, 'gx', 'gy'), may hold values from -4 to 4
- z_directed_motion: float32 [16, 1024, 512], P(None, 'gx', 'gy'), may hold values from -3 to 3
- earlier_rate_change: float32 [16, 1024, 512], P(None, 'gx', 'gy'), may hold values from -6 to 6
- layer_depth_spacing: float32 [16], replicated, may hold values from 0.5 to 2
- backward_spread_ratio: float32 [16], replicated, may hold values from 4 to 100000
- wall_warmth_bounds: float32 [2, 1024, 512], P(None, 'gx', 'gy'), may hold values from -4 to 4
Outputs:
- resulting_warmth_field: float32 [16, 1024, 512], P(None, 'gx', 'gy')
- current_rate_change: float32 [16, 1024, 512], P(None, 'gx', 'gy')
All inputs are finite; a program needn't handle non-finite values.
Results may differ from a plain program's by a relative error of at most 0.000071.
Values sent between devices are 32-bit elements; how exact they have to be, the bound alone decides.
A program may use at most 64 MiB of HBM per device.

v0:
```python
import jax
import jax.numpy as jnp
from jax import lax
from jax.sharding import PartitionSpec as P

COURANT = 0.5
DIFF_Y = 0.2
DIFF_Z = 0.25
NEW_TERM_COEF = 0.75
OLD_TERM_COEF = -5.0 / 12.0


def with_halo(cells, sides, width):
    for axis, dim in sides:
        count = lax.axis_size(axis)
        head = lax.slice_in_dim(cells, 0, width, axis=dim)
        tail = lax.slice_in_dim(cells, cells.shape[dim] - width, cells.shape[dim], axis=dim)
        cells = jnp.concatenate(
            [
                lax.ppermute(tail, axis, [(i, (i + 1) % count) for i in range(count)]),
                cells,
                lax.ppermute(head, axis, [((i + 1) % count, i) for i in range(count)]),
            ],
            axis=dim,
        )
    return cells


def depthwise_rate_change(
    initial_warmth_field, z_directed_motion, layer_depth_spacing, wall_warmth_bounds
):
    inner_face_transport = (
        (z_directed_motion[:-1] + z_directed_motion[1:])
        * (initial_warmth_field[:-1] + initial_warmth_field[1:])
        * 0.25
    )
    empty_layer_sheet = jnp.zeros_like(initial_warmth_field[:1])
    flux_up = jnp.concatenate([empty_layer_sheet, inner_face_transport, empty_layer_sheet], 0)
    spacing = layer_depth_spacing[:, None, None]
    carry_through_depth = (flux_up[1:] - flux_up[:-1]) / spacing
    warmth_with_ghosts = jnp.concatenate(
        [wall_warmth_bounds[:1], initial_warmth_field, wall_warmth_bounds[1:]], 0
    )
    midway_average = jnp.concatenate(
        [
            layer_depth_spacing[:1],
            0.5 * (layer_depth_spacing[:-1] + layer_depth_spacing[1:]),
            layer_depth_spacing[-1:],
        ],
        0,
    )
    gradient_at_faces = (warmth_with_ghosts[1:] - warmth_with_ghosts[:-1]) / midway_average[
        :, None, None
    ]
    thermal_spreading_step = (gradient_at_faces[1:] - gradient_at_faces[:-1]) / spacing
    return (carry_through_depth, thermal_spreading_step)


def reduce_cyclic(values, number):
    margin = jnp.ones_like(number)
    coupling = -number
    saved_levels = []
    current = values
    while current.shape[1] > 1:
        diagonal = margin - 2.0 * coupling
        even_part = current[:, 0::2]
        odd_part = current[:, 1::2]
        saved_levels.append((odd_part, diagonal, coupling))
        current = even_part - coupling / diagonal * (odd_part + jnp.roll(odd_part, 1, axis=1))
        margin = margin * (margin - 4.0 * coupling) / diagonal
        coupling = -(coupling * coupling) / diagonal
    result = current / margin
    for odd_saved, diagonal_saved, coupling_saved in reversed(saved_levels):
        odd_value = (
            odd_saved - coupling_saved * (result + jnp.roll(result, -1, axis=1))
        ) / diagonal_saved
        result = jnp.stack([result, odd_value], axis=2).reshape(
            result.shape[0], 2 * result.shape[1], result.shape[2]
        )
    return result


def on_device(
    initial_warmth_field,
    horizontal_motion_pair,
    z_directed_motion,
    earlier_rate_change,
    layer_depth_spacing,
    backward_spread_ratio,
    wall_warmth_bounds,
):
    warmth_with_margin = with_halo(initial_warmth_field, (("gx", 1), ("gy", 2)), 1)
    flow_pad = with_halo(horizontal_motion_pair, (("gx", 2), ("gy", 3)), 1)
    east_pad = flow_pad[0]
    north_pad = flow_pad[1]
    x_directed_transport = (
        (east_pad[:, :-1, 1:-1] + east_pad[:, 1:, 1:-1])
        * (warmth_with_margin[:, :-1, 1:-1] + warmth_with_margin[:, 1:, 1:-1])
        * 0.25
    )
    y_directed_transport = (
        (north_pad[:, 1:-1, :-1] + north_pad[:, 1:-1, 1:])
        * (warmth_with_margin[:, 1:-1, :-1] + warmth_with_margin[:, 1:-1, 1:])
        * 0.25
    )
    advect_xy = (
        x_directed_transport[:, 1:]
        - x_directed_transport[:, :-1]
        + (y_directed_transport[:, :, 1:] - y_directed_transport[:, :, :-1])
    )
    carry_through_depth, thermal_spreading_step = depthwise_rate_change(
        initial_warmth_field, z_directed_motion, layer_depth_spacing, wall_warmth_bounds
    )
    stacked_layer_count = (
        warmth_with_margin[:, 1:-1, 2:]
        - 2.0 * initial_warmth_field
        + warmth_with_margin[:, 1:-1, :-2]
    )
    current_rate_change = (
        -COURANT * (advect_xy + carry_through_depth)
        + DIFF_Y * stacked_layer_count
        + DIFF_Z * thermal_spreading_step
    )
    linear_system_source = (
        initial_warmth_field
        + NEW_TERM_COEF * current_rate_change
        + OLD_TERM_COEF * earlier_rate_change
    )
    levels_dev = linear_system_source.shape[0] // lax.axis_size("gx")
    first_level = lax.axis_index("gx") * levels_dev
    number = lax.dynamic_slice_in_dim(backward_spread_ratio, first_level, levels_dev)[:, None, None]
    solved_line_values = reduce_cyclic(
        lax.all_to_all(linear_system_source, "gx", split_axis=0, concat_axis=1, tiled=True), number
    )
    resulting_warmth_field = lax.all_to_all(
        solved_line_values, "gx", split_axis=1, concat_axis=0, tiled=True
    )
    return (resulting_warmth_field, current_rate_change)


def solution(mesh):
    in_specs = (
        P(None, "gx", "gy"),
        P(None, None, "gx", "gy"),
        P(None, "gx", "gy"),
        P(None, "gx", "gy"),
        P(),
        P(),
        P(None, "gx", "gy"),
    )
    out_specs = (P(None, "gx", "gy"), P(None, "gx", "gy"))
    return jax.shard_map(
        on_device, mesh=mesh, in_specs=in_specs, out_specs=out_specs, check_vma=False
    )
```

profile of v0, /device:TPU:0, one launch (start us, length us, event | category | flops | bytes accessed | tf_op | source)
XLA Modules:
  0.0 126.3 jit_solution(4332626760719090301)
XLA Ops:
  1.5 3.0 %collective-permute-start.4 = (f32[16,1,128]{2,1,0:T(1,128)S(1)}, f32[16,1,128]{2,1,0:T(1,128)S(1)}, u32[]{:S(2)}, u32[]{:S(2)}) collective-permute-start(f32[16,1,128]{2,1,0:T(1,128)S(1)} %get-tuple-element.45), channel_id=1, source_target_pairs={{0,4},{4,8},{8,12},{12,16},{16,20},{20,24},{24,28},{28,0},{1,5},{5... | collective-permute-start | bytes 24584 | tf_op jit(solution)/shard_map/ppermute | solution.py:20
  4.5 3.1 %collective-permute-start.5 = (f32[16,1,128]{2,1,0:T(1,128)S(1)}, f32[16,1,128]{2,1,0:T(1,128)S(1)}, u32[]{:S(2)}, u32[]{:S(2)}) collective-permute-start(f32[16,1,128]{2,1,0:T(1,128)S(1)} %get-tuple-element.46), channel_id=1, source_target_pairs={{4,0},{8,4},{12,8},{16,12},{20,16},{24,20},{28,24},{0,28},{5,1},{9... | collective-permute-start | bytes 24584 | tf_op jit(solution)/shard_map/ppermute | solution.py:22
  8.7 4.7 %collective-permute-start.1 = (f32[2,16,1,128]{3,2,1,0:T(1,128)S(1)}, f32[2,16,1,128]{3,2,1,0:T(1,128)S(1)}, u32[]{:S(2)}, u32[]{:S(2)}) collective-permute-start(f32[2,16,1,128]{3,2,1,0:T(1,128)S(1)} %get-tuple-element.40), channel_id=1, source_target_pairs={{4,0},{8,4},{12,8},{16,12},{20,16},{24,20},{28,24},{0,28},{5,1},{9... | collective-permute-start | bytes 49160 | tf_op jit(solution)/shard_map/ppermute | solution.py:22
  14.2 1.3 %fusion.115 = (f32[1]{0:T(128)}, f32[1]{0:T(128)}) fusion(f32[16]{0:T(128)} %param.11), kind=kLoop, calls=%fused_computation.186 | loop fusion | bytes 16 | tf_op jit(solution)/shard_map/slice | solution.py:46
  16.4 3.7 %multiply_multiply_fusion = f32[15,128,128]{2,1,0:T(8,128)} fusion(f32[16,128,128]{2,1,0:T(8,128)} %param.7, f32[16,128,128]{2,1,0:T(8,128)} %param.9), kind=kLoop, calls=%fused_computation.32 | loop fusion | flops 983040 | bytes 4915200 | tf_op jit(solution)/shard_map/mul | solution.py:33
  20.3 1.3 %pad_maximum_fusion.14 = f32[17]{0:T(128)S(1)} fusion(f32[1]{0:T(128)} %get-tuple-element.67, f32[15]{0:T(128)S(1)} %add_multiply_fusion, f32[1]{0:T(128)} %get-tuple-element.66), kind=kLoop, calls=%fused_computation.137 | loop fusion | flops 34 | bytes 136 | tf_op jit(solution)/shard_map/concatenate | solution.py:44
  21.6 1.2 fusion.4
  22.9 1.7 %fusion.110 = (f32[16,130,1]{2,1,0:T(8,128)}, f32[16,130,1]{2,1,0:T(8,128)}) fusion(f32[16,130,128]{2,1,0:T(8,128)S(1)} %pad_maximum_fusion.3), kind=kLoop, calls=%fused_computation.181 | loop fusion | bytes 33280 | tf_op jit(solution)/shard_map/slice | solution.py:16
  24.7 2.0 %copy.82 = f32[16,130,1]{1,0,2:T(8,128)S(1)} copy(f32[16,130,1]{2,1,0:T(8,128)} %get-tuple-element.41) | data formatting | bytes 16640 | tf_op jit(solution)/shard_map/slice | solution.py:16
  26.7 1.9 %copy.80 = f32[16,130,1]{1,0,2:T(8,128)S(1)} copy(f32[16,130,1]{2,1,0:T(8,128)} %get-tuple-element.42) | data formatting | bytes 16640 | tf_op jit(solution)/shard_map/slice | solution.py:17
  28.6 1.7 %collective-permute-start.7 = (f32[16,130,1]{1,0,2:T(8,128)S(1)}, f32[16,130,1]{1,0,2:T(8,128)S(1)}, u32[]{:S(2)}, u32[]{:S(2)}) collective-permute-start(f32[16,130,1]{1,0,2:T(8,128)S(1)} %copy.82), channel_id=1, source_target_pairs={{1,0},{2,1},{3,2},{0,3},{5,4},{6,5},{7,6},{4,7},{9,8},{10,9},{11,1... | collective-permute-start | bytes 24968 | tf_op jit(solution)/shard_map/ppermute | solution.py:22
  30.5 2.1 %fusion.108 = (f32[2,16,130,1]{3,2,1,0:T(8,128)}, f32[2,16,130,1]{3,2,1,0:T(8,128)S(1)}) fusion(f32[2,16,130,128]{3,2,1,0:T(8,128)S(1)} %pad_maximum_fusion.1), kind=kLoop, calls=%fused_computation.179 | loop fusion | bytes 66560 | tf_op jit(solution)/shard_map/slice | solution.py:17
  32.6 2.8 %copy.76 = f32[2,16,130,1]{2,1,3,0:T(8,128)S(1)} copy(f32[2,16,130,1]{3,2,1,0:T(8,128)} %get-tuple-element.37) | data formatting | bytes 33280 | tf_op jit(solution)/shard_map/slice | solution.py:17
  35.4 1.2 copy.77
  38.0 2.8 %maximum_maximum_fusion = (f32[16,130,129]{2,1,0:T(8,128)}, f32[16,130,129]{2,1,0:T(8,128)}) fusion(f32[16,1,128]{2,1,0:T(1,128)S(1)} %collective-permute-done.5, f32[16,128,128]{2,1,0:T(8,128)S(1)} %copy-done, f32[16,1,128]{2,1,0:T(1,128)S(1)} %collective-permute-done.4, f32[16,130,1]{2,1,0:T(8,128)S(1)} %copy.81, f32[16,130,1]{2,1,0:T(8,128)S(1)} %copy.83), kind=kLoop, calls=%fused_computation.4 | loop fusion | flops 1609920 | bytes 3228160 | tf_op jit(solution)/shard_map/concatenate | solution.py:18
  40.9 2.2 %copy.78 = f32[2,16,130,1]{3,2,1,0:T(8,128)} copy(f32[2,16,130,1]{2,1,3,0:T(8,128)S(1)} %collective-permute-done.2) | data formatting | bytes 33280 | tf_op jit(solution)/shard_map/ppermute | solution.py:20
  43.1 2.1 %copy.79 = f32[2,16,130,1]{3,2,1,0:T(8,128)} copy(f32[2,16,130,1]{2,1,3,0:T(8,128)S(1)} %collective-permute-done.3) | data formatting | bytes 33280 | tf_op jit(solution)/shard_map/ppermute | solution.py:22
  45.2 4.9 %pad_maximum_fusion = f32[2,16,130,130]{3,2,1,0:T(8,128)S(1)} fusion(f32[2,16,130,1]{3,2,1,0:T(8,128)} %copy.79, f32[2,16,1,128]{3,2,1,0:T(1,128)S(1)} %collective-permute-done.1, f32[2,16,128,128]{3,2,1,0:T(8,128)} %param.8, f32[2,16,1,128]{3,2,1,0:T(1,128)S(1)} %collective-permute-done, f32[2,16,130,1]{3,2,1,0:T(8,128)} %copy.78), kind=kLoop, calls=%fused_computation | loop fusion | flops 2163200 | bytes 4326400 | tf_op jit(solution)/shard_map/concatenate | solution.py:18
  50.4 1.3 %copy-done.3 = f32[16,130,129]{2,1,0:T(8,128)S(1)} copy-done((f32[16,130,129]{2,1,0:T(8,128)S(1)}, f32[16,130,129]{2,1,0:T(8,128)}, u32[]{:S(2)}) %copy-start.3) | copy-done | bytes 1073304
  52.4 1.2 fusion.1
  55.5 2.7 %multiply_add_fusion = (f32[16,128,128]{2,1,0:T(8,128)}, f32[16,128,128]{2,1,0:T(8,128)}) fusion(f32[16,128,128]{2,1,0:T(8,128)S(1)} %copy-done.6, f32[16,128,128]{2,1,0:T(8,128)S(1)} %copy-done, f32[17,128,128]{2,1,0:T(8,128)S(1)} %copy-done.1, f32[16,1,128]{2,1,0:T(1,128)S(1)} %collective-permute-done.5, f32[16,1,128]{2,1,0:T(1,128)S(1)} %collective-permute-done.4, ...), kind=kLoop, calls=%fused_computation.31 | loop fusion | flops 6815744 | bytes 11501888 | tf_op jit(solution)/shard_map/add | solution.py:125
  58.2 3.7 %all-to-all-start = ((f32[16,128,128]{2,1,0:T(8,128)}), f32[16,128,128]{2,1,0:T(8,128)S(1)}, u32[]{:S(2)}, u32[]{:S(2)}) async-start(f32[16,128,128]{2,1,0:T(8,128)} %get-tuple-element.33), calls=%async_computation | async-start | bytes 2097152 | tf_op jit(solution)/shard_map/all_to_all | solution.py:133
  62.1 26.7 %all-to-all-done = f32[16,128,128]{2,1,0:T(8,128)S(1)} async-done(((f32[16,128,128]{2,1,0:T(8,128)}), f32[16,128,128]{2,1,0:T(8,128)S(1)}, u32[]{:S(2)}, u32[]{:S(2)}) %all-to-all-start) | async-done | bytes 1048608 | tf_op jit(solution)/shard_map/all_to_all | solution.py:133
  95.8 29.4 %all_to_all.36 = f32[2,1024,128]{2,0,1:T(2,128)S(1)} all-to-all(f32[2,1024,128]{2,0,1:T(2,128)S(1)} %copy.107), channel_id=1, replica_groups=mesh['gx'=8,'gy'=4] {'gx'}, dimensions={1} | all-to-all | bytes 2097152 | tf_op jit(solution)/shard_map/all_to_all | solution.py:135
  (138 shorter events, 16.2 us)
Async XLA Ops:
  1.5 21.3 %collective-permute-start.4 = (f32[16,1,128]{2,1,0:T(1,128)S(1)}, f32[16,1,128]{2,1,0:T(1,128)S(1)}, u32[]{:S(2)}, u32[]{:S(2)}) collective-permute-start(f32[16,1,128]{2,1,0:T(1,128)S(1)} %get-tuple-element.45), channel_id=1, source_target_pairs={{0,4},{4,8},{8,12},{12,16},{16,20},{20,24},{24,28},{28,0},{1,5},{5... | collective-permute-start | bytes 24584 | tf_op jit(solution)/shard_map/ppermute | solution.py:20
  4.5 18.3 %collective-permute-start.5 = (f32[16,1,128]{2,1,0:T(1,128)S(1)}, f32[16,1,128]{2,1,0:T(1,128)S(1)}, u32[]{:S(2)}, u32[]{:S(2)}) collective-permute-start(f32[16,1,128]{2,1,0:T(1,128)S(1)} %get-tuple-element.46), channel_id=1, source_target_pairs={{4,0},{8,4},{12,8},{16,12},{20,16},{24,20},{28,24},{0,28},{5,1},{9... | collective-permute-start | bytes 24584 | tf_op jit(solution)/shard_map/ppermute | solution.py:22
  8.6 21.7 %collective-permute-start = (f32[2,16,1,128]{3,2,1,0:T(1,128)S(1)}, f32[2,16,1,128]{3,2,1,0:T(1,128)S(1)}, u32[]{:S(2)}, u32[]{:S(2)}) collective-permute-start(f32[2,16,1,128]{3,2,1,0:T(1,128)S(1)} %get-tuple-element.39), channel_id=1, source_target_pairs={{0,4},{4,8},{8,12},{12,16},{16,20},{20,24},{24,28},{28,0},{1,5},{5... | collective-permute-start | bytes 49160 | tf_op jit(solution)/shard_map/ppermute | solution.py:20
  8.7 21.6 %collective-permute-start.1 = (f32[2,16,1,128]{3,2,1,0:T(1,128)S(1)}, f32[2,16,1,128]{3,2,1,0:T(1,128)S(1)}, u32[]{:S(2)}, u32[]{:S(2)}) collective-permute-start(f32[2,16,1,128]{3,2,1,0:T(1,128)S(1)} %get-tuple-element.40), channel_id=1, source_target_pairs={{4,0},{8,4},{12,8},{16,12},{20,16},{24,20},{28,24},{0,28},{5,1},{9... | collective-permute-start | bytes 49160 | tf_op jit(solution)/shard_map/ppermute | solution.py:22
  16.4 3.8 %copy-start.8 = (f32[16]{0:T(128)S(1)}, f32[16]{0:T(128)}, u32[]{:S(2)}) copy-start(f32[16]{0:T(128)} %param.12) | copy-start | bytes 196
  16.4 5.1 %copy-start = (f32[16,128,128]{2,1,0:T(8,128)S(1)}, f32[16,128,128]{2,1,0:T(8,128)}, u32[]{:S(2)}) copy-start(f32[16,128,128]{2,1,0:T(8,128)} %param.7) | copy-start | bytes 3145732
  24.7 5.6 %copy-start.2 = (f32[2,16,128,128]{3,2,1,0:T(8,128)S(1)}, f32[2,16,128,128]{3,2,1,0:T(8,128)}, u32[]{:S(2)}) copy-start(f32[2,16,128,128]{3,2,1,0:T(8,128)} %param.8) | copy-start | bytes 6291460
  28.5 9.1 %collective-permute-start.6 = (f32[16,130,1]{1,0,2:T(8,128)S(1)}, f32[16,130,1]{1,0,2:T(8,128)S(1)}, u32[]{:S(2)}, u32[]{:S(2)}) collective-permute-start(f32[16,130,1]{1,0,2:T(8,128)S(1)} %copy.80), channel_id=1, source_target_pairs={{0,1},{1,2},{2,3},{3,0},{4,5},{5,6},{6,7},{7,4},{8,9},{9,10},{10,1... | collective-permute-start | bytes 24968 | tf_op jit(solution)/shard_map/ppermute | solution.py:20
  28.6 8.6 %collective-permute-start.7 = (f32[16,130,1]{1,0,2:T(8,128)S(1)}, f32[16,130,1]{1,0,2:T(8,128)S(1)}, u32[]{:S(2)}, u32[]{:S(2)}) collective-permute-start(f32[16,130,1]{1,0,2:T(8,128)S(1)} %copy.82), channel_id=1, source_target_pairs={{1,0},{2,1},{3,2},{0,3},{5,4},{6,5},{7,6},{4,7},{9,8},{10,9},{11,1... | collective-permute-start | bytes 24968 | tf_op jit(solution)/shard_map/ppermute | solution.py:22
  36.6 6.4 %collective-permute-start.3 = (f32[2,16,130,1]{2,1,3,0:T(8,128)S(1)}, f32[2,16,130,1]{2,1,3,0:T(8,128)S(1)}, u32[]{:S(2)}, u32[]{:S(2)}) collective-permute-start(f32[2,16,130,1]{2,1,3,0:T(8,128)S(1)} %copy.77), channel_id=1, source_target_pairs={{1,0},{2,1},{3,2},{0,3},{5,4},{6,5},{7,6},{4,7},{9,8},{10,9},{11,1... | collective-permute-start | bytes 49928 | tf_op jit(solution)/shard_map/ppermute | solution.py:22
  36.7 4.2 %collective-permute-start.2 = (f32[2,16,130,1]{2,1,3,0:T(8,128)S(1)}, f32[2,16,130,1]{2,1,3,0:T(8,128)S(1)}, u32[]{:S(2)}, u32[]{:S(2)}) collective-permute-start(f32[2,16,130,1]{2,1,3,0:T(8,128)S(1)} %copy.76), channel_id=1, source_target_pairs={{0,1},{1,2},{2,3},{3,0},{4,5},{5,6},{6,7},{7,4},{8,9},{9,10},{10,1... | collective-permute-start | bytes 49928 | tf_op jit(solution)/shard_map/ppermute | solution.py:20
  50.1 1.6 %copy-start.3 = (f32[16,130,129]{2,1,0:T(8,128)S(1)}, f32[16,130,129]{2,1,0:T(8,128)}, u32[]{:S(2)}) copy-start(f32[16,130,129]{2,1,0:T(8,128)} %get-tuple-element.43) | copy-start | bytes 3219844
  50.1 2.3 %copy-start.4 = (f32[16,130,129]{2,1,0:T(8,128)S(1)}, f32[16,130,129]{2,1,0:T(8,128)}, u32[]{:S(2)}) copy-start(f32[16,130,129]{2,1,0:T(8,128)} %get-tuple-element.44) | copy-start | bytes 3219844
  53.6 1.2 copy-start.1
  53.6 1.5 %copy-start.5 = (f32[15,128,128]{2,1,0:T(8,128)S(1)}, f32[15,128,128]{2,1,0:T(8,128)}, u32[]{:S(2)}) copy-start(f32[15,128,128]{2,1,0:T(8,128)} %multiply_multiply_fusion) | copy-start | bytes 2949124
  53.6 1.8 %copy-start.6 = (f32[16,128,128]{2,1,0:T(8,128)S(1)}, f32[16,128,128]{2,1,0:T(8,128)}, u32[]{:S(2)}) copy-start(f32[16,128,128]{2,1,0:T(8,128)} %param.10) | copy-start | bytes 3145732
  53.6 1.8 %copy-start.7 = (f32[16]{0:T(128)S(1)}, f32[16]{0:T(128)}, u32[]{:S(2)}) copy-start(f32[16]{0:T(128)} %param.11) | copy-start | bytes 196
  58.2 30.6 %all-to-all-start = ((f32[16,128,128]{2,1,0:T(8,128)}), f32[16,128,128]{2,1,0:T(8,128)S(1)}, u32[]{:S(2)}, u32[]{:S(2)}) async-start(f32[16,128,128]{2,1,0:T(8,128)} %get-tuple-element.33), calls=%async_computation | async-start | bytes 2097152 | tf_op jit(solution)/shard_map/all_to_all | solution.py:133
where the time goes:
time: 127 us; the launch traced here: 126 us
  local copies, waits for them, and re-layouts  30.3 us (24%)
  blocking collectives  29.4 us (23%)
  waiting for transfers between devices  26.7 us (21%)
  other arithmetic  21.8 us (17%)
  starting transfers between devices  16.9 us (13%)
    all_to_all x1, blocking collectives, on_device(): lax.all_to_all(solved_line_values, 'gx', split_axis=1, concat_axis=0, til...  29.4 us
    all_to_all x1, waiting for transfers between devices, on_device(): lax.all_to_all(linear_system_source, 'gx', split_axis=0, concat_axis=1, t...  26.7 us
    ppermute x4, starting transfers between devices, with_halo(): lax.ppermute(head, axis, [((i + 1) % count, i) for i in range(count)])  9.59 us
    slice x5, local copies, waits for them, and re-layouts, with_halo(): lax.slice_in_dim(cells, cells.shape[dim] - width, cells.shape[dim], axis=...  8.65 us
    concatenate x4, other arithmetic, with_halo(): jnp.concatenate([lax.ppermute(tail, axis, [(i, (i + 1) % count) for i in...  7.99 us
    slice x3, local copies, waits for them, and re-layouts, with_halo(): head = lax.slice_in_dim(cells, 0, width, axis=dim)  4.93 us
    mul x1, other arithmetic, depthwise_rate_change(): (z_directed_motion[:-1] + z_directed_motion[1:]) * (initial_warmth_field[...  3.74 us
    all_to_all x1, starting transfers between devices, on_device(): lax.all_to_all(linear_system_source, 'gx', split_axis=0, concat_axis=1, t...  3.74 us
  transfers between devices with their start and end apart: 9, of which 1 were waited for; matrix products, arithmetic and copies ran while one was open for 23% of the time, Pallas kernels for 0%

commit v1 on v0

v1 whole, which is shorter than its diff:
```python
import functools

import jax
import jax.numpy as jnp
from jax import lax
from jax.experimental import pallas as pl
from jax.experimental.pallas import tpu as pltpu
from jax.sharding import PartitionSpec as P

COURANT = 0.5
DIFF_Y = 0.2
DIFF_Z = 0.25
NEW_TERM_COEF = 0.75
OLD_TERM_COEF = -5.0 / 12.0

MESH = pl.DeviceIdType.MESH
F32 = jnp.float32
BF16 = jnp.bfloat16
GROUPS = 4


def lanes_of(shape):
    return lax.broadcasted_iota(jnp.int32, shape, len(shape) - 1)


def rows_of(shape):
    return lax.broadcasted_iota(jnp.int32, shape, len(shape) - 2)


def kernel(
    nx, ny, nz, m,
    t_hbm, uv_hbm, w_hbm, old_hbm, dz_ref, r_ref, wall_hbm,
    x_hbm, c_hbm,
    t, uv, w, old, cur, rhs, f_tab, g_tab, green, theta, scale, inv_dz, inv_between,
    pack, pack_got, edge, edge_got, edge_fix, side_fix, moment, moment_got, far,
    in_sem, out_sem, halo_send, halo_recv, moment_send, moment_recv,
):
    gx = lax.axis_index("gx")
    gy = lax.axis_index("gy")
    east, west = lax.rem(gx + 1, nx), lax.rem(gx + nx - 1, nx)
    north, south = lax.rem(gy + 1, ny), lax.rem(gy + ny - 1, ny)
    q_rows = m // 4

    loads = [
        pltpu.make_async_copy(t_hbm, t.at[pl.ds(1, nz)], in_sem.at[0]),
        pltpu.make_async_copy(uv_hbm, uv, in_sem.at[1]),
        pltpu.make_async_copy(wall_hbm.at[pl.ds(0, 1)], t.at[pl.ds(0, 1)], in_sem.at[2]),
        pltpu.make_async_copy(wall_hbm.at[pl.ds(1, 1)], t.at[pl.ds(nz + 1, 1)], in_sem.at[3]),
        pltpu.make_async_copy(w_hbm, w.at[pl.ds(1, nz)], in_sem.at[4]),
        pltpu.make_async_copy(old_hbm, old, in_sem.at[5]),
    ]
    for load in loads:
        load.start()

    barrier = pltpu.get_barrier_semaphore()
    for s in range(1, nx):
        pl.semaphore_signal(
            barrier, inc=1, device_id={"gx": lax.rem(gx + s, nx)}, device_id_type=MESH
        )
    for j in (north, south):
        pl.semaphore_signal(barrier, inc=1, device_id={"gy": j}, device_id_type=MESH)

    for k in range(nz):
        scale[k:k + 1, :] = jnp.full((1, m), r_ref[k], F32)
        inv_dz[k:k + 1, :] = 1.0 / jnp.full((1, m), dz_ref[k], F32)
    inv_between[0:1, :] = inv_dz[0:1, :]
    inv_between[nz:nz + 1, :] = inv_dz[nz - 1:nz, :]
    for k in range(nz - 1):
        inv_between[k + 1:k + 2, :] = 2.0 / jnp.full((1, m), dz_ref[k] + dz_ref[k + 1], F32)
    r = scale[...]
    s = 0.5 / jnp.sqrt(r)
    theta[...] = 2.0 * jnp.log1p(s + s * s / (1.0 + jnp.sqrt(1.0 + s * s)))
    scale[...] = 1.0 / jnp.sqrt(1.0 + 4.0 * r)

    def make_tables(k, carry):
        th = theta[pl.ds(k, 1), :]
        row = rows_of((m, m))
        lane = lanes_of((m, m))
        f_tab[k] = jnp.exp(-th * row.astype(F32))
        g_tab[k] = jnp.exp(-th * (m - 1 - row).astype(F32))
        full = scale[pl.ds(k, 1), :] * jnp.exp(-th * jnp.abs(row - lane).astype(F32))
        high = full.astype(BF16)
        green[k, :, 0:m] = high
        green[k, :, m:2 * m] = (full - high.astype(F32)).astype(BF16)
        return carry

    lax.fori_loop(0, nz, make_tables, 0)

    loads[0].wait()
    loads[1].wait()

    def make_pack(k, carry):
        pt, pv = carry
        pair = lanes_of((q_rows, m)) // 2
        for h in range(4):
            rows = slice(h * q_rows, (h + 1) * q_rows)
            turn = 32 * h + 2 * k + 1
            mine = pair == 16 * h + k
            pt = jnp.where(mine, pltpu.roll(t[k + 1, rows, :], turn, 1), pt)
            pv = jnp.where(mine, pltpu.roll(uv[1, k, rows, :], turn, 1), pv)
        edge[0, 0, pl.ds(k, 1), :] = t[k + 1, m - 1:m, :]
        edge[0, 1, pl.ds(k, 1), :] = uv[0, k, m - 1:m, :]
        edge[1, 0, pl.ds(k, 1), :] = t[k + 1, 0:1, :]
        edge[1, 1, pl.ds(k, 1), :] = uv[0, k, 0:1, :]
        return pt, pv

    blank = jnp.zeros((q_rows, m), F32)
    pt, pv = lax.fori_loop(0, nz, make_pack, (blank, blank))
    pack[0] = pt
    pack[1] = pv

    pl.semaphore_wait(barrier, nx + 1)

    def halo(src, dst, i, where):
        copy = pltpu.make_async_remote_copy(
            src_ref=src, dst_ref=dst, send_sem=halo_send.at[i], recv_sem=halo_recv.at[i],
            device_id=where, device_id_type=MESH,
        )
        copy.start()
        return copy

    halos = [
        halo(pack, pack_got.at[0], 0, {"gy": north}),
        halo(pack, pack_got.at[1], 1, {"gy": south}),
        halo(edge.at[0], edge_got.at[0], 2, {"gx": east}),
        halo(edge.at[1], edge_got.at[1], 3, {"gx": west}),
    ]

    for load in loads[2:]:
        load.wait()
    w[0] = -w[1]
    w[nz + 1] = -w[nz]

    def inner(k, carry):
        row = rows_of((m, m))
        lane = lanes_of((m, m))
        here = t[k + 1]
        u = uv[0, k]
        v = uv[1, k]
        fx = (u + pltpu.roll(u, m - 1, 0)) * (here + pltpu.roll(here, m - 1, 0))
        fx = jnp.where(row == m - 1, 0.0, fx)
        right = pltpu.roll(here, m - 1, 1)
        fy = (v + pltpu.roll(v, m - 1, 1)) * (here + right)
        fy = jnp.where(lane == m - 1, 0.0, fy)
        div = (fx - pltpu.roll(fx, 1, 0)) + (fy - pltpu.roll(fy, 1, 1))
        lap = (
            jnp.where(lane == m - 1, 0.0, right)
            + jnp.where(lane == 0, 0.0, pltpu.roll(here, 1, 1))
            - 2.0 * here
        )
        below, above = t[k], t[k + 2]
        wk = w[k + 1]
        fz = (wk + w[k + 2]) * (here + above) - (w[k] + wk) * (below + here)
        slope = (above - here) * inv_between[pl.ds(k + 1, 1), :] - (here - below) * inv_between[
            pl.ds(k, 1), :
        ]
        idz = inv_dz[pl.ds(k, 1), :]
        value = (
            (-0.25 * COURANT) * (div + fz * idz) + DIFF_Y * lap + DIFF_Z * (slope * idz)
        )
        b = here + NEW_TERM_COEF * value + OLD_TERM_COEF * old[k]
        cur[k] = value
        rhs[k] = b
        moment[0, pl.ds(k, 1), :] = jnp.sum(g_tab[k] * b, axis=0, keepdims=True)
        moment[1, pl.ds(k, 1), :] = jnp.sum(f_tab[k] * b, axis=0, keepdims=True)
        return carry

    lax.fori_loop(0, nz, inner, 0)

    lane1 = lanes_of((1, m))
    th_lane = jnp.zeros((1, m), F32)
    for k in range(nz):
        th_lane = jnp.where(lax.rem(lane1, 32) // 2 == k, theta[k:k + 1, :], th_lane)
    cell = rows_of((q_rows, m)) + (lanes_of((q_rows, m)) // 32) * q_rows
    weight_f = NEW_TERM_COEF * jnp.exp(-th_lane * cell.astype(F32))
    weight_g = NEW_TERM_COEF * jnp.exp(-th_lane * (m - 1 - cell).astype(F32))
    th = theta[...]
    q_end = jnp.exp(-(m - 1.0) * th)

    for copy in halos:
        copy.wait_recv()

    first = lax.rem(lanes_of((q_rows, m)), 2) == 1
    near_t = jnp.where(
        first, pltpu.roll(pack_got[0, 0], 1, 1), pltpu.roll(pack_got[1, 0], m - 1, 1)
    )
    near_v = jnp.where(
        first, pltpu.roll(pack_got[0, 1], 1, 1), pltpu.roll(pack_got[1, 1], m - 1, 1)
    )
    flux = (pack[1] + near_v) * (pack[0] + near_t)
    fix = DIFF_Y * near_t + jnp.where(first, 0.25 * COURANT, -0.25 * COURANT) * flux
    side_fix[...] = fix
    low = (0.25 * COURANT) * (edge_got[0, 1] + edge[1, 1]) * (edge_got[0, 0] + edge[1, 0])
    top = (-0.25 * COURANT) * (edge_got[1, 1] + edge[0, 1]) * (edge_got[1, 0] + edge[0, 0])
    edge_fix[0] = low
    edge_fix[1] = top

    level = rows_of((nz, m))
    lane = lanes_of((nz, m))

    def spread(weights):
        line = jnp.sum(weights * fix, axis=0, keepdims=True)
        line = line + pltpu.roll(line, 32, 1)
        line = line + pltpu.roll(line, 64, 1)
        wide = jnp.broadcast_to(line, (nz, m))
        last = jnp.sum(jnp.where(lane == 2 * level, wide, 0.0), axis=1, keepdims=True)
        head = jnp.sum(jnp.where(lane == 2 * level + 1, wide, 0.0), axis=1, keepdims=True)
        return jnp.where(lane == 0, head, 0.0) + jnp.where(lane == m - 1, last, 0.0)

    moment[0] = moment[0] + NEW_TERM_COEF * (q_end * low + top) + spread(weight_g)
    moment[1] = moment[1] + NEW_TERM_COEF * (low + q_end * top) + spread(weight_f)

    sends = []
    for s in range(1, nx):
        copy = pltpu.make_async_remote_copy(
            src_ref=moment, dst_ref=moment_got.at[s - 1],
            send_sem=moment_send.at[s - 1], recv_sem=moment_recv.at[s - 1],
            device_id={"gx": lax.rem(gx + s, nx)}, device_id_type=MESH,
        )
        copy.start()
        sends.append(copy)

    def local_solve(k, carry):
        lane = lanes_of((q_rows, m))
        row = rows_of((q_rows, m))
        side = (lane == 0) | (lane == m - 1)
        parts = []
        for h in range(4):
            rows = slice(h * q_rows, (h + 1) * q_rows)
            extra = jnp.where(
                side, pltpu.roll(side_fix[...], m - 1 - 32 * h - 2 * k, 1), 0.0
            )
            if h == 0:
                extra = extra + jnp.where(row == 0, edge_fix[0, pl.ds(k, 1), :], 0.0)
            if h == 3:
                extra = extra + jnp.where(row == q_rows - 1, edge_fix[1, pl.ds(k, 1), :], 0.0)
            cur[k, rows, :] = cur[k, rows, :] + extra
            parts.append(rhs[k, rows, :] + NEW_TERM_COEF * extra)
        b = jnp.concatenate(parts, axis=0)
        high = b.astype(BF16)
        pair = jnp.concatenate([high, (b - high.astype(F32)).astype(BF16)], axis=1)
        both = jnp.dot(
            green[k], jnp.concatenate([pair, pair], axis=0), preferred_element_type=F32
        )
        rhs[k] = both[:, 0:m] + both[:, m:2 * m]
        return carry

    per = nz // GROUPS
    stores = []
    for part in range(GROUPS):
        lax.fori_loop(part * per, (part + 1) * per, local_solve, 0)
        span = pl.ds(part * per, per)
        store = pltpu.make_async_copy(cur.at[span], c_hbm.at[span], out_sem.at[part])
        store.start()
        stores.append(store)

    step = jnp.exp(-float(m) * th)
    share = scale[...] * jnp.exp(-th) / (1.0 - jnp.exp(-float(m * nx) * th))
    powers = [jnp.ones_like(step)]
    for s in range(1, nx):
        powers.append(powers[-1] * step)
    from_low = powers[nx - 1] * moment[0]
    from_high = powers[nx - 1] * moment[1]

    for copy in sends:
        copy.wait_recv()
    for s in range(1, nx):
        from_low = from_low + powers[s - 1] * moment_got[s - 1, 0]
        from_high = from_high + powers[nx - s - 1] * moment_got[s - 1, 1]
    far[0] = share * from_low
    far[1] = share * from_high

    def finish(k, carry):
        rhs[k] = (
            rhs[k]
            + f_tab[k] * far[0, pl.ds(k, 1), :]
            + g_tab[k] * far[1, pl.ds(k, 1), :]
        )
        return carry

    for part in range(GROUPS):
        lax.fori_loop(part * per, (part + 1) * per, finish, 0)
        span = pl.ds(part * per, per)
        store = pltpu.make_async_copy(rhs.at[span], x_hbm.at[span], out_sem.at[GROUPS + part])
        store.start()
        stores.append(store)

    for copy in halos + sends:
        copy.wait_send()
    for store in stores:
        store.wait()


def on_device(
    initial_warmth_field,
    horizontal_motion_pair,
    z_directed_motion,
    earlier_rate_change,
    layer_depth_spacing,
    backward_spread_ratio,
    wall_warmth_bounds,
):
    nx = lax.axis_size("gx")
    ny = lax.axis_size("gy")
    nz, m, width = initial_warmth_field.shape
    assert nz == 16 and m == 128 and width == 128
    block = jax.ShapeDtypeStruct((nz, m, m), F32)
    anywhere = pl.BlockSpec(memory_space=pl.ANY)
    scalars = pl.BlockSpec(memory_space=pltpu.SMEM)
    field = pltpu.VMEM((nz, m, m), F32)
    return pl.pallas_call(
        functools.partial(kernel, nx, ny, nz, m),
        out_shape=(block, block),
        in_specs=[anywhere] * 4 + [scalars] * 2 + [anywhere],
        out_specs=(anywhere, anywhere),
        scratch_shapes=[
            pltpu.VMEM((nz + 2, m, m), F32),
            pltpu.VMEM((2, nz, m, m), F32),
            pltpu.VMEM((nz + 2, m, m), F32),
            field, field, field, field, field,
            pltpu.VMEM((nz, m, 2 * m), BF16),
            pltpu.VMEM((nz, m), F32),
            pltpu.VMEM((nz, m), F32),
            pltpu.VMEM((nz, m), F32),
            pltpu.VMEM((nz + 8, m), F32),
            pltpu.VMEM((2, m // 4, m), F32),
            pltpu.VMEM((2, 2, m // 4, m), F32),
            pltpu.VMEM((2, 2, nz, m), F32),
            pltpu.VMEM((2, 2, nz, m), F32),
            pltpu.VMEM((2, nz, m), F32),
            pltpu.VMEM((m // 4, m), F32),
            pltpu.VMEM((2, nz, m), F32),
            pltpu.VMEM((nx - 1, 2, nz, m), F32),
            pltpu.VMEM((2, nz, m), F32),
            pltpu.SemaphoreType.DMA((6,)),
            pltpu.SemaphoreType.DMA((2 * GROUPS,)),
            pltpu.SemaphoreType.DMA((4,)),
            pltpu.SemaphoreType.DMA((4,)),
            pltpu.SemaphoreType.DMA((nx - 1,)),
            pltpu.SemaphoreType.DMA((nx - 1,)),
        ],
        compiler_params=pltpu.CompilerParams(
            collective_id=0, has_side_effects=True, vmem_limit_bytes=40 * 1024 * 1024
        ),
        cost_estimate=pl.CostEstimate(
            flops=16 * 2 * 128 * 256 * 256, bytes_accessed=8 * 1024 * 1024, transcendentals=0
        ),
    )(
        initial_warmth_field,
        horizontal_motion_pair,
        z_directed_motion,
        earlier_rate_change,
        layer_depth_spacing,
        backward_spread_ratio,
        wall_warmth_bounds,
    )


def solution(mesh):
    in_specs = (
        P(None, "gx", "gy"),
        P(None, None, "gx", "gy"),
        P(None, "gx", "gy"),
        P(None, "gx", "gy"),
        P(),
        P(),
        P(None, "gx", "gy"),
    )
    out_specs = (P(None, "gx", "gy"), P(None, "gx", "gy"))
    return jax.shard_map(
        on_device, mesh=mesh, in_specs=in_specs, out_specs=out_specs, check_vma=False
    )
```

time: 127 us -> 26.8 us (0.21)
  blocking collectives: 29.4 us -> 0 us
  waiting for transfers between devices: 26.7 us -> 0 us
  other arithmetic: 21.8 us -> 0 us
  local copies, waits for them, and re-layouts: 30.3 us -> 9.41 us
  starting transfers between devices: 16.9 us -> 0 us
  Pallas kernels: 0 us -> 16.4 us
    all_to_all x1 -> x0, blocking collectives: 29.4 us -> none  [on_device(): lax.all_to_all(solved_line_values, 'gx', split_axis=1, concat_axis=0, til...]
    all_to_all x1 -> x0, waiting for transfers between devices: 26.7 us -> none  [on_device(): lax.all_to_all(linear_system_source, 'gx', split_axis=0, concat_axis=1, t...]
    slice x54 -> x0, local copies, waits for them, and re-layouts: 18 us -> none  [the longest x5 8.65 us: with_halo(): lax.slice_in_dim(cells, cells.shape[dim] - width, cells.shape[dim], axis=...]
    pallas_call x0 -> x1, Pallas kernels: none -> 16.4 us  [on_device(): pl.pallas_call(functools.partial(kernel, nx, ny, nz, m), out_shape=(block...]
    ppermute x8 -> x0, starting transfers between devices: 13.2 us -> none  [the longest x4 9.59 us: with_halo(): lax.ppermute(head, axis, [((i + 1) % count, i) for i in range(count)])]
    concatenate x5 -> x0, other arithmetic: 9.29 us -> none  [the longest x4 7.99 us: with_halo(): jnp.concatenate([lax.ppermute(tail, axis, [(i, (i + 1) % count) for i in...]
    mul x4 -> x0, other arithmetic: 6.42 us -> none  [the longest x1 3.74 us: depthwise_rate_change(): (z_directed_motion[:-1] + z_directed_motion[1:]) * (initial_warmth_field[...]
    unnamed x20 -> x16, local copies, waits for them, and re-layouts: 3.14 us -> 9.41 us
  transfers between devices with their start and end apart: 9 -> 0, of which waited for: 1 -> 0; matrix products, arithmetic and copies ran while one was open for 23% -> 0% of each run, Pallas kernels for 0% -> 0%
where the time goes in v1:
time: 26.8 us; the launch traced here: 26.5 us
  Pallas kernels  16.4 us (61%)
  local copies, waits for them, and re-layouts  9.41 us (35%)
  between operations  0.66 us (2%)
    pallas_call x1, Pallas kernels, on_device(): pl.pallas_call(functools.partial(kernel, nx, ny, nz, m), out_shape=(block...  16.4 us
    unnamed x16, local copies, waits for them, and re-layouts  9.41 us

profile of v1, /device:TPU:0, one launch (start us, length us, event | category | flops | bytes accessed | tf_op | source)
XLA Modules:
  0.0 26.5 jit_solution(9820837420433299687)
XLA Ops:
  0.6 0.0 copy-start
  0.6 1.6 %copy-done = f32[2,16,128,128]{3,2,1,0:T(8,128)S(1)} copy-done((f32[2,16,128,128]{3,2,1,0:T(8,128)S(1)}, f32[2,16,128,128]{3,2,1,0:T(8,128)}, u32[]{:S(2)}) %copy-start) | copy-done | bytes 2097176
  2.2 0.0 copy-start.1
  2.2 1.2 %copy-done.1 = f32[16,128,128]{2,1,0:T(8,128)S(1)} copy-done((f32[16,128,128]{2,1,0:T(8,128)S(1)}, f32[16,128,128]{2,1,0:T(8,128)}, u32[]{:S(2)}) %copy-start.1) | copy-done | bytes 1048600
  3.4 0.0 copy-start.2
  3.5 1.2 %copy-done.2 = f32[16,128,128]{2,1,0:T(8,128)S(1)} copy-done((f32[16,128,128]{2,1,0:T(8,128)S(1)}, f32[16,128,128]{2,1,0:T(8,128)}, u32[]{:S(2)}) %copy-start.2) | copy-done | bytes 1048600
  4.7 0.0 copy-start.3
  4.7 1.2 %copy-done.3 = f32[16,128,128]{2,1,0:T(8,128)S(1)} copy-done((f32[16,128,128]{2,1,0:T(8,128)S(1)}, f32[16,128,128]{2,1,0:T(8,128)}, u32[]{:S(2)}) %copy-start.3) | copy-done | bytes 1048600
  5.9 0.0 copy-start.4
  5.9 0.9 %copy-done.4 = f32[2,128,128]{2,1,0:T(8,128)S(1)} copy-done((f32[2,128,128]{2,1,0:T(8,128)S(1)}, f32[2,128,128]{2,1,0:T(8,128)}, u32[]{:S(2)}) %copy-start.4) | copy-done | bytes 131096
  6.8 0.0 copy-start.5
  6.8 0.7 %copy-done.5 = f32[16]{0:T(128)S(1)} copy-done((f32[16]{0:T(128)S(1)}, f32[16]{0:T(128)}, u32[]{:S(2)}) %copy-start.5) | copy-done | bytes 88
  7.5 0.0 copy-start.6
  7.5 0.7 %copy-done.6 = f32[16]{0:T(128)S(1)} copy-done((f32[16]{0:T(128)S(1)}, f32[16]{0:T(128)}, u32[]{:S(2)}) %copy-start.6) | copy-done | bytes 88
  8.1 16.4 %shard_map.86 = (f32[16,128,128]{2,1,0:T(8,128)S(1)}, f32[16,128,128]{2,1,0:T(8,128)S(1)}) custom-call(f32[16,128,128]{2,1,0:T(8,128)S(1)} %copy-done.1, f32[2,16,128,128]{3,2,1,0:T(8,128)S(1)} %copy-done, f32[16,128,128]{2,1,0:T(8,128)S(1)} %copy-done.2, f32[16,128,128]{2,1,0:T(8,128)S(1)} %copy-done.3, f32[16]{0:T(128)S(1)} %copy-done.5, f32[16]{0:T(128)S(1)} %copy-done.6, ...), custom_call_target="tpu_custom_call" | custom-call | flops 268435456 | bytes 8388608 | tf_op jit(solution)/shard_map/pallas_call | solution.py:311
  24.6 1.0 %copy.11 = f32[16,128,128]{2,1,0:T(8,128)} copy(f32[16,128,128]{2,1,0:T(8,128)S(1)} %get-tuple-element.4) | data formatting | bytes 2097152
  25.5 1.0 %copy.12 = f32[16,128,128]{2,1,0:T(8,128)} copy(f32[16,128,128]{2,1,0:T(8,128)S(1)} %get-tuple-element.5) | data formatting | bytes 2097152
Async XLA Ops:
  0.6 1.6 %copy-start = (f32[2,16,128,128]{3,2,1,0:T(8,128)S(1)}, f32[2,16,128,128]{3,2,1,0:T(8,128)}, u32[]{:S(2)}) copy-start(f32[2,16,128,128]{3,2,1,0:T(8,128)} %uv_hbm.1) | copy-start | bytes 6291460
  2.2 1.2 %copy-start.1 = (f32[16,128,128]{2,1,0:T(8,128)S(1)}, f32[16,128,128]{2,1,0:T(8,128)}, u32[]{:S(2)}) copy-start(f32[16,128,128]{2,1,0:T(8,128)} %t_hbm.1) | copy-start | bytes 3145732
  3.4 1.2 %copy-start.2 = (f32[16,128,128]{2,1,0:T(8,128)S(1)}, f32[16,128,128]{2,1,0:T(8,128)}, u32[]{:S(2)}) copy-start(f32[16,128,128]{2,1,0:T(8,128)} %w_hbm.1) | copy-start | bytes 3145732
  4.7 1.2 %copy-start.3 = (f32[16,128,128]{2,1,0:T(8,128)S(1)}, f32[16,128,128]{2,1,0:T(8,128)}, u32[]{:S(2)}) copy-start(f32[16,128,128]{2,1,0:T(8,128)} %old_hbm.1) | copy-start | bytes 3145732
  5.9 0.9 %copy-start.4 = (f32[2,128,128]{2,1,0:T(8,128)S(1)}, f32[2,128,128]{2,1,0:T(8,128)}, u32[]{:S(2)}) copy-start(f32[2,128,128]{2,1,0:T(8,128)} %wall_hbm.1) | copy-start | bytes 393220
  6.8 0.7 %copy-start.5 = (f32[16]{0:T(128)S(1)}, f32[16]{0:T(128)}, u32[]{:S(2)}) copy-start(f32[16]{0:T(128)} %dz_ref.1) | copy-start | bytes 196
  7.5 0.7 %copy-start.6 = (f32[16]{0:T(128)S(1)}, f32[16]{0:T(128)}, u32[]{:S(2)}) copy-start(f32[16]{0:T(128)} %r_ref.1) | copy-start | bytes 196

commit v2 on v1

--- a/solution.py
+++ b/solution.py
@@ -17,6 +17,7 @@
 F32 = jnp.float32
 BF16 = jnp.bfloat16
 GROUPS = 4
+OFF = 8
 
 
 def lanes_of(shape):
@@ -29,10 +30,12 @@
 
 def kernel(
     nx, ny, nz, m,
-    t_hbm, uv_hbm, w_hbm, old_hbm, dz_ref, r_ref, wall_hbm,
+    t_hbm, uv_hbm, w_hbm, old_hbm, dz_hbm, r_hbm, wall_hbm,
     x_hbm, c_hbm,
-    t, uv, w, old, cur, rhs, f_tab, g_tab, green, theta, scale, inv_dz, inv_between,
-    pack, pack_got, edge, edge_got, edge_fix, side_fix, moment, moment_got, far,
+    t, u_all, v_all, w, old, cur, rhs, green, head_pow, tail_pow, block_pow, far_block,
+    theta, scale, inv_dz, up_coef, down_coef,
+    pack, pack_got, edge, edge_got, edge_fix, side_fix, moment, moment_got,
+    dz_ref, r_ref,
     in_sem, out_sem, halo_send, halo_recv, moment_send, moment_recv,
 ):
     gx = lax.axis_index("gx")
@@ -40,14 +43,19 @@
     east, west = lax.rem(gx + 1, nx), lax.rem(gx + nx - 1, nx)
     north, south = lax.rem(gy + 1, ny), lax.rem(gy + ny - 1, ny)
     q_rows = m // 4
+    blocks = m // 8
+    inside = pl.ds(OFF, m)
 
     loads = [
-        pltpu.make_async_copy(t_hbm, t.at[pl.ds(1, nz)], in_sem.at[0]),
-        pltpu.make_async_copy(uv_hbm, uv, in_sem.at[1]),
-        pltpu.make_async_copy(wall_hbm.at[pl.ds(0, 1)], t.at[pl.ds(0, 1)], in_sem.at[2]),
-        pltpu.make_async_copy(wall_hbm.at[pl.ds(1, 1)], t.at[pl.ds(nz + 1, 1)], in_sem.at[3]),
-        pltpu.make_async_copy(w_hbm, w.at[pl.ds(1, nz)], in_sem.at[4]),
-        pltpu.make_async_copy(old_hbm, old, in_sem.at[5]),
+        pltpu.make_async_copy(r_hbm, r_ref, in_sem.at[0]),
+        pltpu.make_async_copy(dz_hbm, dz_ref, in_sem.at[1]),
+        pltpu.make_async_copy(t_hbm, t.at[pl.ds(1, nz), inside], in_sem.at[2]),
+        pltpu.make_async_copy(uv_hbm.at[1], v_all, in_sem.at[3]),
+        pltpu.make_async_copy(uv_hbm.at[0], u_all.at[:, inside], in_sem.at[4]),
+        pltpu.make_async_copy(wall_hbm.at[0], t.at[0, inside], in_sem.at[5]),
+        pltpu.make_async_copy(wall_hbm.at[1], t.at[nz + 1, inside], in_sem.at[6]),
+        pltpu.make_async_copy(w_hbm, w.at[pl.ds(1, nz)], in_sem.at[7]),
+        pltpu.make_async_copy(old_hbm, old, in_sem.at[8]),
     ]
     for load in loads:
         load.start()
@@ -60,48 +68,72 @@
     for j in (north, south):
         pl.semaphore_signal(barrier, inc=1, device_id={"gy": j}, device_id_type=MESH)
 
+    loads[0].wait()
+    loads[1].wait()
     for k in range(nz):
         scale[k:k + 1, :] = jnp.full((1, m), r_ref[k], F32)
         inv_dz[k:k + 1, :] = 1.0 / jnp.full((1, m), dz_ref[k], F32)
-    inv_between[0:1, :] = inv_dz[0:1, :]
-    inv_between[nz:nz + 1, :] = inv_dz[nz - 1:nz, :]
+    down_coef[0:1, :] = inv_dz[0:1, :]
+    up_coef[nz - 1:nz, :] = inv_dz[nz - 1:nz, :]
     for k in range(nz - 1):
-        inv_between[k + 1:k + 2, :] = 2.0 / jnp.full((1, m), dz_ref[k] + dz_ref[k + 1], F32)
+        between = 2.0 / jnp.full((1, m), dz_ref[k] + dz_ref[k + 1], F32)
+        up_coef[k:k + 1, :] = between
+        down_coef[k + 1:k + 2, :] = between
+    up_coef[...] = DIFF_Z * up_coef[...] * inv_dz[...]
+    down_coef[...] = DIFF_Z * down_coef[...] * inv_dz[...]
+    inv_dz[...] = (-0.25 * COURANT) * inv_dz[...]
     r = scale[...]
     s = 0.5 / jnp.sqrt(r)
     theta[...] = 2.0 * jnp.log1p(s + s * s / (1.0 + jnp.sqrt(1.0 + s * s)))
     scale[...] = 1.0 / jnp.sqrt(1.0 + 4.0 * r)
+    th = theta[...]
+    for b in range(blocks):
+        block_pow[b] = jnp.exp((-8.0 * b) * th)
 
     def make_tables(k, carry):
+        row = rows_of((8, m))
+        lane = lanes_of((8, m))
         th = theta[pl.ds(k, 1), :]
-        row = rows_of((m, m))
-        lane = lanes_of((m, m))
-        f_tab[k] = jnp.exp(-th * row.astype(F32))
-        g_tab[k] = jnp.exp(-th * (m - 1 - row).astype(F32))
-        full = scale[pl.ds(k, 1), :] * jnp.exp(-th * jnp.abs(row - lane).astype(F32))
-        high = full.astype(BF16)
-        green[k, :, 0:m] = high
-        green[k, :, m:2 * m] = (full - high.astype(F32)).astype(BF16)
+        head_pow[k] = jnp.exp(-th * row.astype(F32))
+        tail_pow[k] = jnp.exp(-th * (7 - row).astype(F32))
+        level_scale = scale[pl.ds(k, 1), :]
+        near = level_scale * jnp.exp(-th * jnp.abs(row - lane).astype(F32))
+        wrap = level_scale * jnp.exp(-th * (row - lane + m).astype(F32))
+        for b in range(0, blocks, 2):
+            full = jnp.concatenate(
+                [
+                    pltpu.roll(jnp.where(lane < m - 8 * c, near, wrap), 8 * c, 1)
+                    if c
+                    else near
+                    for c in (b, b + 1)
+                ],
+                axis=0,
+            )
+            high = full.astype(BF16)
+            green[k, 8 * b:8 * b + 16, 0:m] = high
+            green[k, 8 * b:8 * b + 16, m:2 * m] = (full - high.astype(F32)).astype(BF16)
         return carry
 
     lax.fori_loop(0, nz, make_tables, 0)
 
-    loads[0].wait()
-    loads[1].wait()
+    for load in loads[2:5]:
+        load.wait()
 
     def make_pack(k, carry):
         pt, pv = carry
         pair = lanes_of((q_rows, m)) // 2
         for h in range(4):
-            rows = slice(h * q_rows, (h + 1) * q_rows)
             turn = 32 * h + 2 * k + 1
             mine = pair == 16 * h + k
-            pt = jnp.where(mine, pltpu.roll(t[k + 1, rows, :], turn, 1), pt)
-            pv = jnp.where(mine, pltpu.roll(uv[1, k, rows, :], turn, 1), pv)
-        edge[0, 0, pl.ds(k, 1), :] = t[k + 1, m - 1:m, :]
-        edge[0, 1, pl.ds(k, 1), :] = uv[0, k, m - 1:m, :]
-        edge[1, 0, pl.ds(k, 1), :] = t[k + 1, 0:1, :]
-        edge[1, 1, pl.ds(k, 1), :] = uv[0, k, 0:1, :]
+            here = t[k + 1, OFF + h * q_rows:OFF + (h + 1) * q_rows, :]
+            pt = jnp.where(mine, pltpu.roll(here, turn, 1), pt)
+            pv = jnp.where(
+                mine, pltpu.roll(v_all[k, h * q_rows:(h + 1) * q_rows, :], turn, 1), pv
+            )
+        edge[0, 0, pl.ds(k, 1), :] = t[k + 1, OFF + m - 1:OFF + m, :]
+        edge[0, 1, pl.ds(k, 1), :] = u_all[k, OFF + m - 1:OFF + m, :]
+        edge[1, 0, pl.ds(k, 1), :] = t[k + 1, OFF:OFF + 1, :]
+        edge[1, 1, pl.ds(k, 1), :] = u_all[k, OFF:OFF + 1, :]
         return pt, pv
 
     blank = jnp.zeros((q_rows, m), F32)
@@ -126,43 +158,58 @@
         halo(edge.at[1], edge_got.at[1], 3, {"gx": west}),
     ]
 
-    for load in loads[2:]:
+    for load in loads[5:]:
         load.wait()
     w[0] = -w[1]
     w[nz + 1] = -w[nz]
 
     def inner(k, carry):
-        row = rows_of((m, m))
-        lane = lanes_of((m, m))
-        here = t[k + 1]
-        u = uv[0, k]
-        v = uv[1, k]
-        fx = (u + pltpu.roll(u, m - 1, 0)) * (here + pltpu.roll(here, m - 1, 0))
-        fx = jnp.where(row == m - 1, 0.0, fx)
-        right = pltpu.roll(here, m - 1, 1)
-        fy = (v + pltpu.roll(v, m - 1, 1)) * (here + right)
-        fy = jnp.where(lane == m - 1, 0.0, fy)
-        div = (fx - pltpu.roll(fx, 1, 0)) + (fy - pltpu.roll(fy, 1, 1))
-        lap = (
-            jnp.where(lane == m - 1, 0.0, right)
-            + jnp.where(lane == 0, 0.0, pltpu.roll(here, 1, 1))
-            - 2.0 * here
-        )
-        below, above = t[k], t[k + 2]
-        wk = w[k + 1]
-        fz = (wk + w[k + 2]) * (here + above) - (w[k] + wk) * (below + here)
-        slope = (above - here) * inv_between[pl.ds(k + 1, 1), :] - (here - below) * inv_between[
-            pl.ds(k, 1), :
-        ]
-        idz = inv_dz[pl.ds(k, 1), :]
-        value = (
-            (-0.25 * COURANT) * (div + fz * idz) + DIFF_Y * lap + DIFF_Z * (slope * idz)
-        )
-        b = here + NEW_TERM_COEF * value + OLD_TERM_COEF * old[k]
-        cur[k] = value
-        rhs[k] = b
-        moment[0, pl.ds(k, 1), :] = jnp.sum(g_tab[k] * b, axis=0, keepdims=True)
-        moment[1, pl.ds(k, 1), :] = jnp.sum(f_tab[k] * b, axis=0, keepdims=True)
+        row = rows_of((q_rows, m))
+        lane = lanes_of((q_rows, m))
+        one = pl.ds(k, 1)
+        up, down, idz = up_coef[one, :], down_coef[one, :], inv_dz[one, :]
+        low_sum = jnp.zeros((8, m), F32)
+        high_sum = jnp.zeros((8, m), F32)
+        for h in range(4):
+            rows = slice(h * q_rows, (h + 1) * q_rows)
+            pad = slice(OFF + h * q_rows, OFF + (h + 1) * q_rows)
+            after = slice(OFF + h * q_rows + 1, OFF + (h + 1) * q_rows + 1)
+            before = slice(OFF + h * q_rows - 1, OFF + (h + 1) * q_rows - 1)
+            here = t[k + 1, pad, :]
+            u = u_all[k, pad, :]
+            v = v_all[k, rows, :]
+            fx = (u + u_all[k, after, :]) * (here + t[k + 1, after, :])
+            gx_flux = (u_all[k, before, :] + u) * (t[k + 1, before, :] + here)
+            if h == 3:
+                fx = jnp.where(row == q_rows - 1, 0.0, fx)
+            if h == 0:
+                gx_flux = jnp.where(row == 0, 0.0, gx_flux)
+            right = pltpu.roll(here, m - 1, 1)
+            fy = (v + pltpu.roll(v, m - 1, 1)) * (here + right)
+            fy = jnp.where(lane == m - 1, 0.0, fy)
+            div = (fx - gx_flux) + (fy - pltpu.roll(fy, 1, 1))
+            lap = jnp.where(lane == m - 1, 0.0, right) + jnp.where(
+                lane == 0, 0.0, pltpu.roll(here, 1, 1)
+            )
+            below, above = t[k, pad, :], t[k + 2, pad, :]
+            wk = w[k + 1, rows, :]
+            fz = (wk + w[k + 2, rows, :]) * (here + above) - (w[k, rows, :] + wk) * (below + here)
+            value = (
+                (-0.25 * COURANT) * div
+                + idz * fz
+                + DIFF_Y * (lap - 2.0 * here)
+                + (up * (above - here) - down * (here - below))
+            )
+            b = here + NEW_TERM_COEF * value + OLD_TERM_COEF * old[k, rows, :]
+            cur[k, rows, :] = value
+            rhs[k, rows, :] = b
+            for i in range(4):
+                c = 4 * h + i
+                part = b[8 * i:8 * i + 8, :]
+                low_sum = low_sum + block_pow[blocks - 1 - c, one, :] * part
+                high_sum = high_sum + block_pow[c, one, :] * part
+        moment[0, one, :] = jnp.sum(tail_pow[k] * low_sum, axis=0, keepdims=True)
+        moment[1, one, :] = jnp.sum(head_pow[k] * high_sum, axis=0, keepdims=True)
         return carry
 
     lax.fori_loop(0, nz, inner, 0)
@@ -174,7 +221,6 @@
     cell = rows_of((q_rows, m)) + (lanes_of((q_rows, m)) // 32) * q_rows
     weight_f = NEW_TERM_COEF * jnp.exp(-th_lane * cell.astype(F32))
     weight_g = NEW_TERM_COEF * jnp.exp(-th_lane * (m - 1 - cell).astype(F32))
-    th = theta[...]
     q_end = jnp.exp(-(m - 1.0) * th)
 
     for copy in halos:
@@ -267,15 +313,22 @@
     for s in range(1, nx):
         from_low = from_low + powers[s - 1] * moment_got[s - 1, 0]
         from_high = from_high + powers[nx - s - 1] * moment_got[s - 1, 1]
-    far[0] = share * from_low
-    far[1] = share * from_high
+    from_low = share * from_low
+    from_high = share * from_high
+    for b in range(blocks):
+        far_block[0, b] = block_pow[b] * from_low
+        far_block[1, b] = block_pow[blocks - 1 - b] * from_high
 
     def finish(k, carry):
-        rhs[k] = (
-            rhs[k]
-            + f_tab[k] * far[0, pl.ds(k, 1), :]
-            + g_tab[k] * far[1, pl.ds(k, 1), :]
-        )
+        head = head_pow[k]
+        tail = tail_pow[k]
+        for b in range(blocks):
+            rows = slice(8 * b, 8 * b + 8)
+            rhs[k, rows, :] = (
+                rhs[k, rows, :]
+                + head * far_block[0, b, pl.ds(k, 1), :]
+                + tail * far_block[1, b, pl.ds(k, 1), :]
+            )
         return carry
 
     for part in range(GROUPS):
@@ -306,23 +359,26 @@
     assert nz == 16 and m == 128 and width == 128
     block = jax.ShapeDtypeStruct((nz, m, m), F32)
     anywhere = pl.BlockSpec(memory_space=pl.ANY)
-    scalars = pl.BlockSpec(memory_space=pltpu.SMEM)
+    far_away = pl.BlockSpec(memory_space=pltpu.HBM)
     field = pltpu.VMEM((nz, m, m), F32)
+    row = pltpu.VMEM((nz, m), F32)
     return pl.pallas_call(
         functools.partial(kernel, nx, ny, nz, m),
         out_shape=(block, block),
-        in_specs=[anywhere] * 4 + [scalars] * 2 + [anywhere],
+        in_specs=[far_away] * 7,
         out_specs=(anywhere, anywhere),
         scratch_shapes=[
+            pltpu.VMEM((nz + 2, m + 2 * OFF, m), F32),
+            pltpu.VMEM((nz, m + 2 * OFF, m), F32),
+            field,
             pltpu.VMEM((nz + 2, m, m), F32),
-            pltpu.VMEM((2, nz, m, m), F32),
-            pltpu.VMEM((nz + 2, m, m), F32),
-            field, field, field, field, field,
+            field, field, field,
             pltpu.VMEM((nz, m, 2 * m), BF16),
-            pltpu.VMEM((nz, m), F32),
-            pltpu.VMEM((nz, m), F32),
-            pltpu.VMEM((nz, m), F32),
-            pltpu.VMEM((nz + 8, m), F32),
+            pltpu.VMEM((nz, 8, m), F32),
+            pltpu.VMEM((nz, 8, m), F32),
+            pltpu.VMEM((m // 8, nz, m), F32),
+            pltpu.VMEM((2, m // 8, nz, m), F32),
+            row, row, row, row, row,
             pltpu.VMEM((2, m // 4, m), F32),
             pltpu.VMEM((2, 2, m // 4, m), F32),
             pltpu.VMEM((2, 2, nz, m), F32),
@@ -331,8 +387,9 @@
             pltpu.VMEM((m // 4, m), F32),
             pltpu.VMEM((2, nz, m), F32),
             pltpu.VMEM((nx - 1, 2, nz, m), F32),
-            pltpu.VMEM((2, nz, m), F32),
-            pltpu.SemaphoreType.DMA((6,)),
+            pltpu.SMEM((nz,), F32),
+            pltpu.SMEM((nz,), F32),
+            pltpu.SemaphoreType.DMA((9,)),
             pltpu.SemaphoreType.DMA((2 * GROUPS,)),
             pltpu.SemaphoreType.DMA((4,)),
             pltpu.SemaphoreType.DMA((4,)),
@@ -340,7 +397,7 @@
             pltpu.SemaphoreType.DMA((nx - 1,)),
         ],
         compiler_params=pltpu.CompilerParams(
-            collective_id=0, has_side_effects=True, vmem_limit_bytes=40 * 1024 * 1024
+            collective_id=0, has_side_effects=True, vmem_limit_bytes=60 * 1024 * 1024
         ),
         cost_estimate=pl.CostEstimate(
             flops=16 * 2 * 128 * 256 * 256, bytes_accessed=8 * 1024 * 1024, transcendentals=0

time: 26.8 us -> 21.8 us (0.81)
  local copies, waits for them, and re-layouts: 9.41 us -> 3.36 us
  Pallas kernels: 16.4 us -> 17.6 us
    unnamed x16 -> x4, local copies, waits for them, and re-layouts: 9.41 us -> 3.36 us
    pallas_call x1, Pallas kernels: 16.4 us -> 17.6 us  [on_device(): pl.pallas_call(functools.partial(kernel, nx, ny, nz, m), out_shape=(block...]
where the time goes in v2:
time: 21.8 us; the launch traced here: 21.6 us
  Pallas kernels  17.6 us (81%)
  local copies, waits for them, and re-layouts  3.36 us (15%)
  between operations  0.65 us (3%)
    pallas_call x1, Pallas kernels, on_device(): pl.pallas_call(functools.partial(kernel, nx, ny, nz, m), out_shape=(block...  17.6 us
    unnamed x4, local copies, waits for them, and re-layouts  3.36 us

profile of v2, /device:TPU:0, one launch (start us, length us, event | category | flops | bytes accessed | tf_op | source)
XLA Modules:
  0.0 21.6 jit_solution(3460911757885459093)
XLA Ops:
  0.6 17.6 %shard_map.86 = (f32[16,128,128]{2,1,0:T(8,128)}, f32[16,128,128]{2,1,0:T(8,128)}) custom-call(f32[16,128,128]{2,1,0:T(8,128)} %t_hbm.1, f32[2,16,128,128]{3,2,1,0:T(8,128)} %uv_hbm.1, f32[16,128,128]{2,1,0:T(8,128)} %w_hbm.1, f32[16,128,128]{2,1,0:T(8,128)} %old_hbm.1, f32[16]{0:T(128)} %dz_hbm.1, f32[16]{0:T(128)} %r_hbm.1, f32[2,128,128]{2,1,0:T(8,128)} %wall_hbm.1), custom_call_target="tpu_custom_call" | custom-call | flops 268435456 | bytes 8388608 | tf_op jit(solution)/shard_map/pallas_call | solution.py:365
  18.2 0.0 copy-start
  18.2 2.4 %copy.11 = f32[16,128,128]{2,1,0:T(8,128)} copy(f32[16,128,128]{2,1,0:T(8,128)} %get-tuple-element.4) | data formatting | bytes 2097152
  20.6 0.0 copy-done
  20.6 1.0 %copy.12 = f32[16,128,128]{2,1,0:T(8,128)} copy(f32[16,128,128]{2,1,0:T(8,128)S(1)} %copy-done) | data formatting | bytes 2097152
Async XLA Ops:
  18.2 2.4 %copy-start = (f32[16,128,128]{2,1,0:T(8,128)S(1)}, f32[16,128,128]{2,1,0:T(8,128)}, u32[]{:S(2)}) copy-start(f32[16,128,128]{2,1,0:T(8,128)} %get-tuple-element.5) | copy-start | bytes 3145732

commit v3 on v2

--- a/solution.py
+++ b/solution.py
@@ -20,6 +20,15 @@
 OFF = 8
 
 
+def each_level(start, stop, step, body, carry):
+    def together(i, carry):
+        for j in range(step):
+            carry = body(start + i * step + j, carry)
+        return carry
+
+    return lax.fori_loop(0, (stop - start) // step, together, carry)
+
+
 def lanes_of(shape):
     return lax.broadcasted_iota(jnp.int32, shape, len(shape) - 1)
 
@@ -34,7 +43,7 @@
     x_hbm, c_hbm,
     t, u_all, v_all, w, old, cur, rhs, green, head_pow, tail_pow, block_pow, far_block,
     theta, scale, inv_dz, up_coef, down_coef,
-    pack, pack_got, edge, edge_got, edge_fix, side_fix, moment, moment_got,
+    pack, pack_got, edge, edge_got, edge_fix, side_fix, moment, moment_got, eights,
     dz_ref, r_ref,
     in_sem, out_sem, halo_send, halo_recv, moment_send, moment_recv,
 ):
@@ -114,7 +123,7 @@
             green[k, 8 * b:8 * b + 16, m:2 * m] = (full - high.astype(F32)).astype(BF16)
         return carry
 
-    lax.fori_loop(0, nz, make_tables, 0)
+    each_level(0, nz, 4, make_tables, 0)
 
     for load in loads[2:5]:
         load.wait()
@@ -137,7 +146,7 @@
         return pt, pv
 
     blank = jnp.zeros((q_rows, m), F32)
-    pt, pv = lax.fori_loop(0, nz, make_pack, (blank, blank))
+    pt, pv = each_level(0, nz, 4, make_pack, (blank, blank))
     pack[0] = pt
     pack[1] = pv
 
@@ -208,11 +217,11 @@
                 part = b[8 * i:8 * i + 8, :]
                 low_sum = low_sum + block_pow[blocks - 1 - c, one, :] * part
                 high_sum = high_sum + block_pow[c, one, :] * part
-        moment[0, one, :] = jnp.sum(tail_pow[k] * low_sum, axis=0, keepdims=True)
-        moment[1, one, :] = jnp.sum(head_pow[k] * high_sum, axis=0, keepdims=True)
+        eights[0, k] = tail_pow[k] * low_sum
+        eights[1, k] = head_pow[k] * high_sum
         return carry
 
-    lax.fori_loop(0, nz, inner, 0)
+    each_level(0, nz, 2, inner, 0)
 
     lane1 = lanes_of((1, m))
     th_lane = jnp.zeros((1, m), F32)
@@ -222,6 +231,8 @@
     weight_f = NEW_TERM_COEF * jnp.exp(-th_lane * cell.astype(F32))
     weight_g = NEW_TERM_COEF * jnp.exp(-th_lane * (m - 1 - cell).astype(F32))
     q_end = jnp.exp(-(m - 1.0) * th)
+    sums_low = jnp.sum(eights[0], axis=1)
+    sums_high = jnp.sum(eights[1], axis=1)
 
     for copy in halos:
         copy.wait_recv()
@@ -253,8 +264,8 @@
         head = jnp.sum(jnp.where(lane == 2 * level + 1, wide, 0.0), axis=1, keepdims=True)
         return jnp.where(lane == 0, head, 0.0) + jnp.where(lane == m - 1, last, 0.0)
 
-    moment[0] = moment[0] + NEW_TERM_COEF * (q_end * low + top) + spread(weight_g)
-    moment[1] = moment[1] + NEW_TERM_COEF * (low + q_end * top) + spread(weight_f)
+    moment[0] = sums_low + NEW_TERM_COEF * (q_end * low + top) + spread(weight_g)
+    moment[1] = sums_high + NEW_TERM_COEF * (low + q_end * top) + spread(weight_f)
 
     sends = []
     for s in range(1, nx):
@@ -294,7 +305,7 @@
     per = nz // GROUPS
     stores = []
     for part in range(GROUPS):
-        lax.fori_loop(part * per, (part + 1) * per, local_solve, 0)
+        each_level(part * per, (part + 1) * per, per, local_solve, 0)
         span = pl.ds(part * per, per)
         store = pltpu.make_async_copy(cur.at[span], c_hbm.at[span], out_sem.at[part])
         store.start()
@@ -332,7 +343,7 @@
         return carry
 
     for part in range(GROUPS):
-        lax.fori_loop(part * per, (part + 1) * per, finish, 0)
+        each_level(part * per, (part + 1) * per, per, finish, 0)
         span = pl.ds(part * per, per)
         store = pltpu.make_async_copy(rhs.at[span], x_hbm.at[span], out_sem.at[GROUPS + part])
         store.start()
@@ -387,6 +398,7 @@
             pltpu.VMEM((m // 4, m), F32),
             pltpu.VMEM((2, nz, m), F32),
             pltpu.VMEM((nx - 1, 2, nz, m), F32),
+            pltpu.VMEM((2, nz, 8, m), F32),
             pltpu.SMEM((nz,), F32),
             pltpu.SMEM((nz,), F32),
             pltpu.SemaphoreType.DMA((9,)),

time: 21.8 us -> 20.2 us (0.927)
  Pallas kernels: 17.6 us -> 16 us
    pallas_call x1, Pallas kernels: 17.6 us -> 16 us  [on_device(): pl.pallas_call(functools.partial(kernel, nx, ny, nz, m), out_shape=(block...]
where the time goes in v3:
time: 20.2 us; the launch traced here: 20 us
  Pallas kernels  16 us (79%)
  local copies, waits for them, and re-layouts  3.36 us (17%)
  between operations  0.65 us (3%)
    pallas_call x1, Pallas kernels, on_device(): pl.pallas_call(functools.partial(kernel, nx, ny, nz, m), out_shape=(block...  16 us
    unnamed x4, local copies, waits for them, and re-layouts  3.36 us

profile of v3, /device:TPU:0, one launch (start us, length us, event | category | flops | bytes accessed | tf_op | source)
XLA Modules:
  0.0 20.0 jit_solution(10474419864506939195)
XLA Ops:
  0.6 16.0 %shard_map.86 = (f32[16,128,128]{2,1,0:T(8,128)}, f32[16,128,128]{2,1,0:T(8,128)}) custom-call(f32[16,128,128]{2,1,0:T(8,128)} %t_hbm.1, f32[2,16,128,128]{3,2,1,0:T(8,128)} %uv_hbm.1, f32[16,128,128]{2,1,0:T(8,128)} %w_hbm.1, f32[16,128,128]{2,1,0:T(8,128)} %old_hbm.1, f32[16]{0:T(128)} %dz_hbm.1, f32[16]{0:T(128)} %r_hbm.1, f32[2,128,128]{2,1,0:T(8,128)} %wall_hbm.1), custom_call_target="tpu_custom_call" | custom-call | flops 268435456 | bytes 8388608 | tf_op jit(solution)/shard_map/pallas_call | solution.py:376
  16.6 0.0 copy-start
  16.6 2.4 %copy.11 = f32[16,128,128]{2,1,0:T(8,128)} copy(f32[16,128,128]{2,1,0:T(8,128)} %get-tuple-element.4) | data formatting | bytes 2097152
  19.0 0.0 copy-done
  19.0 1.0 %copy.12 = f32[16,128,128]{2,1,0:T(8,128)} copy(f32[16,128,128]{2,1,0:T(8,128)S(1)} %copy-done) | data formatting | bytes 2097152
Async XLA Ops:
  16.6 2.4 %copy-start = (f32[16,128,128]{2,1,0:T(8,128)S(1)}, f32[16,128,128]{2,1,0:T(8,128)}, u32[]{:S(2)}) copy-start(f32[16,128,128]{2,1,0:T(8,128)} %get-tuple-element.5) | copy-start | bytes 3145732

commit v4 on v3

--- a/solution.py
+++ b/solution.py
@@ -40,12 +40,12 @@
 def kernel(
     nx, ny, nz, m,
     t_hbm, uv_hbm, w_hbm, old_hbm, dz_hbm, r_hbm, wall_hbm,
-    x_hbm, c_hbm,
-    t, u_all, v_all, w, old, cur, rhs, green, head_pow, tail_pow, block_pow, far_block,
+    rhs, cur, head_pow, tail_pow, far_block,
+    t, u_all, v_all, w, old, green, block_pow,
     theta, scale, inv_dz, up_coef, down_coef,
     pack, pack_got, edge, edge_got, edge_fix, side_fix, moment, moment_got, eights,
     dz_ref, r_ref,
-    in_sem, out_sem, halo_send, halo_recv, moment_send, moment_recv,
+    in_sem, halo_send, halo_recv, moment_send, moment_recv,
 ):
     gx = lax.axis_index("gx")
     gy = lax.axis_index("gy")
@@ -302,14 +302,7 @@
         rhs[k] = both[:, 0:m] + both[:, m:2 * m]
         return carry
 
-    per = nz // GROUPS
-    stores = []
-    for part in range(GROUPS):
-        each_level(part * per, (part + 1) * per, per, local_solve, 0)
-        span = pl.ds(part * per, per)
-        store = pltpu.make_async_copy(cur.at[span], c_hbm.at[span], out_sem.at[part])
-        store.start()
-        stores.append(store)
+    each_level(0, nz, 4, local_solve, 0)
 
     step = jnp.exp(-float(m) * th)
     share = scale[...] * jnp.exp(-th) / (1.0 - jnp.exp(-float(m * nx) * th))
@@ -330,27 +323,34 @@
         far_block[0, b] = block_pow[b] * from_low
         far_block[1, b] = block_pow[blocks - 1 - b] * from_high
 
+    for copy in halos + sends:
+        copy.wait_send()
+
+
+def finish_kernel(nz, m, part_ref, cur_ref, head_pow, tail_pow, far_block, x_hbm, c_hbm, x, out_sem):
+    blocks = m // 8
+    stores = [pltpu.make_async_copy(cur_ref, c_hbm, out_sem.at[GROUPS])]
+    stores[0].start()
+
     def finish(k, carry):
         head = head_pow[k]
         tail = tail_pow[k]
         for b in range(blocks):
             rows = slice(8 * b, 8 * b + 8)
-            rhs[k, rows, :] = (
-                rhs[k, rows, :]
+            x[k, rows, :] = (
+                part_ref[k, rows, :]
                 + head * far_block[0, b, pl.ds(k, 1), :]
                 + tail * far_block[1, b, pl.ds(k, 1), :]
             )
         return carry
 
+    per = nz // GROUPS
     for part in range(GROUPS):
         each_level(part * per, (part + 1) * per, per, finish, 0)
         span = pl.ds(part * per, per)
-        store = pltpu.make_async_copy(rhs.at[span], x_hbm.at[span], out_sem.at[GROUPS + part])
+        store = pltpu.make_async_copy(x.at[span], x_hbm.at[span], out_sem.at[part])
         store.start()
         stores.append(store)
-
-    for copy in halos + sends:
-        copy.wait_send()
     for store in stores:
         store.wait()
 
@@ -373,22 +373,27 @@
     far_away = pl.BlockSpec(memory_space=pltpu.HBM)
     field = pltpu.VMEM((nz, m, m), F32)
     row = pltpu.VMEM((nz, m), F32)
-    return pl.pallas_call(
+    near = pl.BlockSpec(memory_space=pltpu.VMEM)
+    carried = (
+        field,
+        field,
+        pltpu.VMEM((nz, 8, m), F32),
+        pltpu.VMEM((nz, 8, m), F32),
+        pltpu.VMEM((2, m // 8, nz, m), F32),
+    )
+    between = pl.pallas_call(
         functools.partial(kernel, nx, ny, nz, m),
-        out_shape=(block, block),
+        out_shape=carried,
         in_specs=[far_away] * 7,
-        out_specs=(anywhere, anywhere),
+        out_specs=(near,) * 5,
         scratch_shapes=[
             pltpu.VMEM((nz + 2, m + 2 * OFF, m), F32),
             pltpu.VMEM((nz, m + 2 * OFF, m), F32),
             field,
             pltpu.VMEM((nz + 2, m, m), F32),
-            field, field, field,
+            field,
             pltpu.VMEM((nz, m, 2 * m), BF16),
-            pltpu.VMEM((nz, 8, m), F32),
-            pltpu.VMEM((nz, 8, m), F32),
             pltpu.VMEM((m // 8, nz, m), F32),
-            pltpu.VMEM((2, m // 8, nz, m), F32),
             row, row, row, row, row,
             pltpu.VMEM((2, m // 4, m), F32),
             pltpu.VMEM((2, 2, m // 4, m), F32),
@@ -402,14 +407,13 @@
             pltpu.SMEM((nz,), F32),
             pltpu.SMEM((nz,), F32),
             pltpu.SemaphoreType.DMA((9,)),
-            pltpu.SemaphoreType.DMA((2 * GROUPS,)),
             pltpu.SemaphoreType.DMA((4,)),
             pltpu.SemaphoreType.DMA((4,)),
             pltpu.SemaphoreType.DMA((nx - 1,)),
             pltpu.SemaphoreType.DMA((nx - 1,)),
         ],
         compiler_params=pltpu.CompilerParams(
-            collective_id=0, has_side_effects=True, vmem_limit_bytes=60 * 1024 * 1024
+            collective_id=0, has_side_effects=True, vmem_limit_bytes=58 * 1024 * 1024
         ),
         cost_estimate=pl.CostEstimate(
             flops=16 * 2 * 128 * 256 * 256, bytes_accessed=8 * 1024 * 1024, transcendentals=0
@@ -423,6 +427,14 @@
         backward_spread_ratio,
         wall_warmth_bounds,
     )
+    return pl.pallas_call(
+        functools.partial(finish_kernel, nz, m),
+        out_shape=(block, block),
+        in_specs=[near] * 5,
+        out_specs=(anywhere, anywhere),
+        scratch_shapes=[field, pltpu.SemaphoreType.DMA((GROUPS + 1,))],
+        compiler_params=pltpu.CompilerParams(vmem_limit_bytes=16 * 1024 * 1024),
+    )(*between)
 
 
 def solution(mesh):

time: 20.2 us -> 17.1 us (0.85)
  local copies, waits for them, and re-layouts: 3.36 us -> 0 us
  Pallas kernels: 16 us -> 16.3 us
    unnamed x4 -> x0, local copies, waits for them, and re-layouts: 3.36 us -> none
    pallas_call x1 -> x2, Pallas kernels: 16 us -> 16.3 us  [the longest x1 14.9 us: on_device(): pl.pallas_call(functools.partial(kernel, nx, ny, nz, m), out_shape=carrie...]
where the time goes in v4:
time: 17.1 us; the launch traced here: 16.9 us
  Pallas kernels  16.3 us (95%)
  between operations  0.64 us (4%)
    pallas_call x1, Pallas kernels, on_device(): pl.pallas_call(functools.partial(kernel, nx, ny, nz, m), out_shape=carrie...  14.9 us
    pallas_call x1, Pallas kernels, on_device(): pl.pallas_call(functools.partial(finish_kernel, nz, m), out_shape=(block,...  1.35 us

profile of v4, /device:TPU:0, one launch (start us, length us, event | category | flops | bytes accessed | tf_op | source)
XLA Modules:
  0.0 16.9 jit_solution(8742753580965817577)
XLA Ops:
  0.6 14.9 %shard_map.86 = (f32[16,128,128]{2,1,0:T(8,128)S(1)}, f32[16,128,128]{2,1,0:T(8,128)S(1)}, f32[16,8,128]{2,1,0:T(8,128)S(1)}, f32[16,8,128]{2,1,0:T(8,128)S(1)}, f32[2,16,16,128]{3,2,1,0:T(8,128)S(1)}) custom-call(f32[16,128,128]{2,1,0:T(8,128)} %t_hbm.1, f32[2,16,128,128]{3,2,1,0:T(8,128)} %uv_hbm.1, f32[16,128,128]{2,1,0:T(8,128)} %w_hbm.1, ...), custom_call_target="tpu_custom_call" | custom-call | flops 268435456 | bytes 8388608 | tf_op jit(solution)/shard_map/pallas_call | solution.py:384
  15.6 1.4 %shard_map.87 = (f32[16,128,128]{2,1,0:T(8,128)}, f32[16,128,128]{2,1,0:T(8,128)}) custom-call(f32[16,128,128]{2,1,0:T(8,128)S(1)} %get-tuple-element.7.part_ref, f32[16,128,128]{2,1,0:T(8,128)S(1)} %get-tuple-element.8.cur_ref, f32[16,8,128]{2,1,0:T(8,128)S(1)} %get-tuple-element.9.head_pow, f32[16,8,128]{2,1,0:T(8,128)S(1)} %get-tuple-element.10.tail_pow, ...), custom_call_target="tpu_custom_call" | custom-call | tf_op jit(solution)/shard_map/pallas_call | solution.py:430

commit v5 on v4

--- a/solution.py
+++ b/solution.py
@@ -76,6 +76,48 @@
         )
     for j in (north, south):
         pl.semaphore_signal(barrier, inc=1, device_id={"gy": j}, device_id_type=MESH)
+
+    for load in loads[2:5]:
+        load.wait()
+
+    def make_pack(k, carry):
+        pt, pv = carry
+        pair = lanes_of((q_rows, m)) // 2
+        for h in range(4):
+            turn = 32 * h + 2 * k + 1
+            mine = pair == 16 * h + k
+            here = t[k + 1, OFF + h * q_rows:OFF + (h + 1) * q_rows, :]
+            pt = jnp.where(mine, pltpu.roll(here, turn, 1), pt)
+            pv = jnp.where(
+                mine, pltpu.roll(v_all[k, h * q_rows:(h + 1) * q_rows, :], turn, 1), pv
+            )
+        edge[0, 0, pl.ds(k, 1), :] = t[k + 1, OFF + m - 1:OFF + m, :]
+        edge[0, 1, pl.ds(k, 1), :] = u_all[k, OFF + m - 1:OFF + m, :]
+        edge[1, 0, pl.ds(k, 1), :] = t[k + 1, OFF:OFF + 1, :]
+        edge[1, 1, pl.ds(k, 1), :] = u_all[k, OFF:OFF + 1, :]
+        return pt, pv
+
+    blank = jnp.zeros((q_rows, m), F32)
+    pt, pv = each_level(0, nz, 4, make_pack, (blank, blank))
+    pack[0] = pt
+    pack[1] = pv
+
+    pl.semaphore_wait(barrier, nx + 1)
+
+    def halo(src, dst, i, where):
+        copy = pltpu.make_async_remote_copy(
+            src_ref=src, dst_ref=dst, send_sem=halo_send.at[i], recv_sem=halo_recv.at[i],
+            device_id=where, device_id_type=MESH,
+        )
+        copy.start()
+        return copy
+
+    halos = [
+        halo(pack, pack_got.at[0], 0, {"gy": north}),
+        halo(pack, pack_got.at[1], 1, {"gy": south}),
+        halo(edge.at[0], edge_got.at[0], 2, {"gx": east}),
+        halo(edge.at[1], edge_got.at[1], 3, {"gx": west}),
+    ]
 
     loads[0].wait()
     loads[1].wait()
@@ -105,67 +147,9 @@
         th = theta[pl.ds(k, 1), :]
         head_pow[k] = jnp.exp(-th * row.astype(F32))
         tail_pow[k] = jnp.exp(-th * (7 - row).astype(F32))
-        level_scale = scale[pl.ds(k, 1), :]
-        near = level_scale * jnp.exp(-th * jnp.abs(row - lane).astype(F32))
-        wrap = level_scale * jnp.exp(-th * (row - lane + m).astype(F32))
-        for b in range(0, blocks, 2):
-            full = jnp.concatenate(
-                [
-                    pltpu.roll(jnp.where(lane < m - 8 * c, near, wrap), 8 * c, 1)
-                    if c
-                    else near
-                    for c in (b, b + 1)
-                ],
-                axis=0,
-            )
-            high = full.astype(BF16)
-            green[k, 8 * b:8 * b + 16, 0:m] = high
-            green[k, 8 * b:8 * b + 16, m:2 * m] = (full - high.astype(F32)).astype(BF16)
         return carry
 
     each_level(0, nz, 4, make_tables, 0)
-
-    for load in loads[2:5]:
-        load.wait()
-
-    def make_pack(k, carry):
-        pt, pv = carry
-        pair = lanes_of((q_rows, m)) // 2
-        for h in range(4):
-            turn = 32 * h + 2 * k + 1
-            mine = pair == 16 * h + k
-            here = t[k + 1, OFF + h * q_rows:OFF + (h + 1) * q_rows, :]
-            pt = jnp.where(mine, pltpu.roll(here, turn, 1), pt)
-            pv = jnp.where(
-                mine, pltpu.roll(v_all[k, h * q_rows:(h + 1) * q_rows, :], turn, 1), pv
-            )
-        edge[0, 0, pl.ds(k, 1), :] = t[k + 1, OFF + m - 1:OFF + m, :]
-        edge[0, 1, pl.ds(k, 1), :] = u_all[k, OFF + m - 1:OFF + m, :]
-        edge[1, 0, pl.ds(k, 1), :] = t[k + 1, OFF:OFF + 1, :]
-        edge[1, 1, pl.ds(k, 1), :] = u_all[k, OFF:OFF + 1, :]
-        return pt, pv
-
-    blank = jnp.zeros((q_rows, m), F32)
-    pt, pv = each_level(0, nz, 4, make_pack, (blank, blank))
-    pack[0] = pt
-    pack[1] = pv
-
-    pl.semaphore_wait(barrier, nx + 1)
-
-    def halo(src, dst, i, where):
-        copy = pltpu.make_async_remote_copy(
-            src_ref=src, dst_ref=dst, send_sem=halo_send.at[i], recv_sem=halo_recv.at[i],
-            device_id=where, device_id_type=MESH,
-        )
-        copy.start()
-        return copy
-
-    halos = [
-        halo(pack, pack_got.at[0], 0, {"gy": north}),
-        halo(pack, pack_got.at[1], 1, {"gy": south}),
-        halo(edge.at[0], edge_got.at[0], 2, {"gx": east}),
-        halo(edge.at[1], edge_got.at[1], 3, {"gx": west}),
-    ]
 
     for load in loads[5:]:
         load.wait()
@@ -221,7 +205,7 @@
         eights[1, k] = head_pow[k] * high_sum
         return carry
 
-    each_level(0, nz, 2, inner, 0)
+    each_level(0, nz, 4, inner, 0)
 
     lane1 = lanes_of((1, m))
     th_lane = jnp.zeros((1, m), F32)
@@ -276,6 +260,30 @@
         )
         copy.start()
         sends.append(copy)
+
+    def local_inverse(k, carry):
+        row8 = rows_of((8, m))
+        lane8 = lanes_of((8, m))
+        th = theta[pl.ds(k, 1), :]
+        level_scale = scale[pl.ds(k, 1), :]
+        near = level_scale * jnp.exp(-th * jnp.abs(row8 - lane8).astype(F32))
+        wrap = level_scale * jnp.exp(-th * (row8 - lane8 + m).astype(F32))
+        for b0 in range(0, blocks, 2):
+            full = jnp.concatenate(
+                [
+                    pltpu.roll(jnp.where(lane8 < m - 8 * c, near, wrap), 8 * c, 1)
+                    if c
+                    else near
+                    for c in (b0, b0 + 1)
+                ],
+                axis=0,
+            )
+            high = full.astype(BF16)
+            green[k, 8 * b0:8 * b0 + 16, 0:m] = high
+            green[k, 8 * b0:8 * b0 + 16, m:2 * m] = (full - high.astype(F32)).astype(BF16)
+        return carry
+
+    each_level(0, nz, 4, local_inverse, 0)
 
     def local_solve(k, carry):
         lane = lanes_of((q_rows, m))

time: 17.1 us -> 17.1 us (level)
  no operation moved by 1% of the time
where the time goes in v5:
time: 17.1 us; the launch traced here: 16.9 us
  Pallas kernels  16.3 us (95%)
  between operations  0.64 us (4%)
    pallas_call x1, Pallas kernels, on_device(): pl.pallas_call(functools.partial(kernel, nx, ny, nz, m), out_shape=carrie...  14.9 us
    pallas_call x1, Pallas kernels, on_device(): pl.pallas_call(functools.partial(finish_kernel, nz, m), out_shape=(block,...  1.35 us

profile of v5, /device:TPU:0, one launch (start us, length us, event | category | flops | bytes accessed | tf_op | source)
XLA Modules:
  0.0 16.9 jit_solution(4703467807625882014)
XLA Ops:
  0.6 14.9 %shard_map.86 = (f32[16,128,128]{2,1,0:T(8,128)S(1)}, f32[16,128,128]{2,1,0:T(8,128)S(1)}, f32[16,8,128]{2,1,0:T(8,128)S(1)}, f32[16,8,128]{2,1,0:T(8,128)S(1)}, f32[2,16,16,128]{3,2,1,0:T(8,128)S(1)}) custom-call(f32[16,128,128]{2,1,0:T(8,128)} %t_hbm.1, f32[2,16,128,128]{3,2,1,0:T(8,128)} %uv_hbm.1, f32[16,128,128]{2,1,0:T(8,128)} %w_hbm.1, ...), custom_call_target="tpu_custom_call" | custom-call | flops 268435456 | bytes 8388608 | tf_op jit(solution)/shard_map/pallas_call | solution.py:392
  15.6 1.4 %shard_map.87 = (f32[16,128,128]{2,1,0:T(8,128)}, f32[16,128,128]{2,1,0:T(8,128)}) custom-call(f32[16,128,128]{2,1,0:T(8,128)S(1)} %get-tuple-element.7.part_ref, f32[16,128,128]{2,1,0:T(8,128)S(1)} %get-tuple-element.8.cur_ref, f32[16,8,128]{2,1,0:T(8,128)S(1)} %get-tuple-element.9.head_pow, f32[16,8,128]{2,1,0:T(8,128)S(1)} %get-tuple-element.10.tail_pow, ...), custom_call_target="tpu_custom_call" | custom-call | tf_op jit(solution)/shard_map/pallas_call | solution.py:438

commit v6 on v4

--- a/solution.py
+++ b/solution.py
@@ -43,9 +43,9 @@
     rhs, cur, head_pow, tail_pow, far_block,
     t, u_all, v_all, w, old, green, block_pow,
     theta, scale, inv_dz, up_coef, down_coef,
-    pack, pack_got, edge, edge_got, edge_fix, side_fix, moment, moment_got, eights,
+    pack, pack_got, edge, edge_got, edge_fix, side_fix, moment, moment_got, shares, far, far_got, eights,
     dz_ref, r_ref,
-    in_sem, halo_send, halo_recv, moment_send, moment_recv,
+    in_sem, halo_send, halo_recv, moment_send, moment_recv, far_send, far_recv,
 ):
     gx = lax.axis_index("gx")
     gy = lax.axis_index("gy")
@@ -53,6 +53,7 @@
     north, south = lax.rem(gy + 1, ny), lax.rem(gy + ny - 1, ny)
     q_rows = m // 4
     blocks = m // 8
+    lv = nz // nx
     inside = pl.ds(OFF, m)
 
     loads = [
@@ -105,22 +106,6 @@
         th = theta[pl.ds(k, 1), :]
         head_pow[k] = jnp.exp(-th * row.astype(F32))
         tail_pow[k] = jnp.exp(-th * (7 - row).astype(F32))
-        level_scale = scale[pl.ds(k, 1), :]
-        near = level_scale * jnp.exp(-th * jnp.abs(row - lane).astype(F32))
-        wrap = level_scale * jnp.exp(-th * (row - lane + m).astype(F32))
-        for b in range(0, blocks, 2):
-            full = jnp.concatenate(
-                [
-                    pltpu.roll(jnp.where(lane < m - 8 * c, near, wrap), 8 * c, 1)
-                    if c
-                    else near
-                    for c in (b, b + 1)
-                ],
-                axis=0,
-            )
-            high = full.astype(BF16)
-            green[k, 8 * b:8 * b + 16, 0:m] = high
-            green[k, 8 * b:8 * b + 16, m:2 * m] = (full - high.astype(F32)).astype(BF16)
         return carry
 
     each_level(0, nz, 4, make_tables, 0)
@@ -221,7 +206,7 @@
         eights[1, k] = head_pow[k] * high_sum
         return carry
 
-    each_level(0, nz, 2, inner, 0)
+    each_level(0, nz, 4, inner, 0)
 
     lane1 = lanes_of((1, m))
     th_lane = jnp.zeros((1, m), F32)
@@ -264,18 +249,79 @@
         head = jnp.sum(jnp.where(lane == 2 * level + 1, wide, 0.0), axis=1, keepdims=True)
         return jnp.where(lane == 0, head, 0.0) + jnp.where(lane == m - 1, last, 0.0)
 
-    moment[0] = sums_low + NEW_TERM_COEF * (q_end * low + top) + spread(weight_g)
-    moment[1] = sums_high + NEW_TERM_COEF * (low + q_end * top) + spread(weight_f)
+    own_low = sums_low + NEW_TERM_COEF * (q_end * low + top) + spread(weight_g)
+    own_high = sums_high + NEW_TERM_COEF * (low + q_end * top) + spread(weight_f)
+    for q in range(nx):
+        moment[q, 0:lv, :] = own_low[q * lv:(q + 1) * lv, :]
+        moment[q, lv:2 * lv, :] = own_high[q * lv:(q + 1) * lv, :]
 
     sends = []
     for s in range(1, nx):
+        there = lax.rem(gx + s, nx)
         copy = pltpu.make_async_remote_copy(
-            src_ref=moment, dst_ref=moment_got.at[s - 1],
-            send_sem=moment_send.at[s - 1], recv_sem=moment_recv.at[s - 1],
-            device_id={"gx": lax.rem(gx + s, nx)}, device_id_type=MESH,
+            src_ref=moment.at[there], dst_ref=moment_got.at[s],
+            send_sem=moment_send.at[s], recv_sem=moment_recv.at[s],
+            device_id={"gx": there}, device_id_type=MESH,
         )
         copy.start()
         sends.append(copy)
+
+    step = jnp.exp(-float(m) * th)
+    share = scale[...] * jnp.exp(-th) / (1.0 - jnp.exp(-float(m * nx) * th))
+    for q in range(nx):
+        shares[q, 0:lv, :] = share[q * lv:(q + 1) * lv, :]
+        shares[q, lv:2 * lv, :] = step[q * lv:(q + 1) * lv, :]
+
+    def local_inverse(k, carry):
+        row8 = rows_of((8, m))
+        lane8 = lanes_of((8, m))
+        th = theta[pl.ds(k, 1), :]
+        level_scale = scale[pl.ds(k, 1), :]
+        near = level_scale * jnp.exp(-th * jnp.abs(row8 - lane8).astype(F32))
+        wrap = level_scale * jnp.exp(-th * (row8 - lane8 + m).astype(F32))
+        for b0 in range(0, blocks, 2):
+            full = jnp.concatenate(
+                [
+                    pltpu.roll(jnp.where(lane8 < m - 8 * c, near, wrap), 8 * c, 1)
+                    if c
+                    else near
+                    for c in (b0, b0 + 1)
+                ],
+                axis=0,
+            )
+            high = full.astype(BF16)
+            green[k, 8 * b0:8 * b0 + 16, 0:m] = high
+            green[k, 8 * b0:8 * b0 + 16, m:2 * m] = (full - high.astype(F32)).astype(BF16)
+        return carry
+
+    each_level(0, nz, 4, local_inverse, 0)
+
+    for copy in sends:
+        copy.wait_recv()
+    mine = shares[gx]
+    powers = [mine[0:lv, :]]
+    for s in range(1, nx):
+        powers.append(powers[-1] * mine[lv:2 * lv, :])
+    lows = [moment[gx, 0:lv, :]] + [moment_got[s, 0:lv, :] for s in range(1, nx)]
+    highs = [moment[gx, lv:2 * lv, :]] + [moment_got[s, lv:2 * lv, :] for s in range(1, nx)]
+    returns = []
+    for e in range(nx):
+        from_low = jnp.zeros((lv, m), F32)
+        from_high = jnp.zeros((lv, m), F32)
+        for s in range(1, nx + 1):
+            from_low = from_low + powers[s - 1] * lows[(s - e) % nx]
+            from_high = from_high + powers[s - 1] * highs[(-s - e) % nx]
+        far[e, 0:lv, :] = from_low
+        far[e, lv:2 * lv, :] = from_high
+        if e:
+            copy = pltpu.make_async_remote_copy(
+                src_ref=far.at[e], dst_ref=far_got.at[gx],
+                send_sem=far_send.at[e], recv_sem=far_recv.at[e],
+                device_id={"gx": lax.rem(gx + e, nx)}, device_id_type=MESH,
+            )
+            copy.start()
+            returns.append(copy)
+    far_got[gx] = far[0]
 
     def local_solve(k, carry):
         lane = lanes_of((q_rows, m))
@@ -304,26 +350,15 @@
 
     each_level(0, nz, 4, local_solve, 0)
 
-    step = jnp.exp(-float(m) * th)
-    share = scale[...] * jnp.exp(-th) / (1.0 - jnp.exp(-float(m * nx) * th))
-    powers = [jnp.ones_like(step)]
-    for s in range(1, nx):
-        powers.append(powers[-1] * step)
-    from_low = powers[nx - 1] * moment[0]
-    from_high = powers[nx - 1] * moment[1]
-
-    for copy in sends:
+    for copy in returns:
         copy.wait_recv()
-    for s in range(1, nx):
-        from_low = from_low + powers[s - 1] * moment_got[s - 1, 0]
-        from_high = from_high + powers[nx - s - 1] * moment_got[s - 1, 1]
-    from_low = share * from_low
-    from_high = share * from_high
+    from_low = jnp.concatenate([far_got[q, 0:lv, :] for q in range(nx)], axis=0)
+    from_high = jnp.concatenate([far_got[q, lv:2 * lv, :] for q in range(nx)], axis=0)
     for b in range(blocks):
         far_block[0, b] = block_pow[b] * from_low
         far_block[1, b] = block_pow[blocks - 1 - b] * from_high
 
-    for copy in halos + sends:
+    for copy in halos + sends + returns:
         copy.wait_send()
 
 
@@ -373,6 +408,8 @@
     far_away = pl.BlockSpec(memory_space=pltpu.HBM)
     field = pltpu.VMEM((nz, m, m), F32)
     row = pltpu.VMEM((nz, m), F32)
+    by_owner = pltpu.VMEM((nx, 2 * (nz // nx), m), F32)
+    each_peer = pltpu.SemaphoreType.DMA((nx,))
     near = pl.BlockSpec(memory_space=pltpu.VMEM)
     carried = (
         field,
@@ -401,16 +438,14 @@
             pltpu.VMEM((2, 2, nz, m), F32),
             pltpu.VMEM((2, nz, m), F32),
             pltpu.VMEM((m // 4, m), F32),
-            pltpu.VMEM((2, nz, m), F32),
-            pltpu.VMEM((nx - 1, 2, nz, m), F32),
+            by_owner, by_owner, by_owner, by_owner, by_owner,
             pltpu.VMEM((2, nz, 8, m), F32),
             pltpu.SMEM((nz,), F32),
             pltpu.SMEM((nz,), F32),
             pltpu.SemaphoreType.DMA((9,)),
             pltpu.SemaphoreType.DMA((4,)),
             pltpu.SemaphoreType.DMA((4,)),
-            pltpu.SemaphoreType.DMA((nx - 1,)),
-            pltpu.SemaphoreType.DMA((nx - 1,)),
+            each_peer, each_peer, each_peer, each_peer,
         ],
         compiler_params=pltpu.CompilerParams(
             collective_id=0, has_side_effects=True, vmem_limit_bytes=58 * 1024 * 1024

time: 17.1 us -> 21.3 us (1.25)
  Pallas kernels: 16.3 us -> 20.5 us
    pallas_call x1, Pallas kernels: 14.9 us -> 19.2 us  [on_device(): pl.pallas_call(functools.partial(kernel, nx, ny, nz, m), out_shape=carrie...]
where the time goes in v6:
time: 21.3 us; the launch traced here: 21.2 us
  Pallas kernels  20.5 us (96%)
  between operations  0.64 us (3%)
    pallas_call x1, Pallas kernels, on_device(): pl.pallas_call(functools.partial(kernel, nx, ny, nz, m), out_shape=carrie...  19.2 us
    pallas_call x1, Pallas kernels, on_device(): pl.pallas_call(functools.partial(finish_kernel, nz, m), out_shape=(block,...  1.35 us

profile of v6, /device:TPU:0, one launch (start us, length us, event | category | flops | bytes accessed | tf_op | source)
XLA Modules:
  0.0 21.2 jit_solution(10299889182634546286)
XLA Ops:
  0.6 19.2 %shard_map.86 = (f32[16,128,128]{2,1,0:T(8,128)S(1)}, f32[16,128,128]{2,1,0:T(8,128)S(1)}, f32[16,8,128]{2,1,0:T(8,128)S(1)}, f32[16,8,128]{2,1,0:T(8,128)S(1)}, f32[2,16,16,128]{3,2,1,0:T(8,128)S(1)}) custom-call(f32[16,128,128]{2,1,0:T(8,128)} %t_hbm.1, f32[2,16,128,128]{3,2,1,0:T(8,128)} %uv_hbm.1, f32[16,128,128]{2,1,0:T(8,128)} %w_hbm.1, ...), custom_call_target="tpu_custom_call" | custom-call | flops 268435456 | bytes 8388608 | tf_op jit(solution)/shard_map/pallas_call | solution.py:421
  19.8 1.4 %shard_map.87 = (f32[16,128,128]{2,1,0:T(8,128)}, f32[16,128,128]{2,1,0:T(8,128)}) custom-call(f32[16,128,128]{2,1,0:T(8,128)S(1)} %get-tuple-element.7.part_ref, f32[16,128,128]{2,1,0:T(8,128)S(1)} %get-tuple-element.8.cur_ref, f32[16,8,128]{2,1,0:T(8,128)S(1)} %get-tuple-element.9.head_pow, f32[16,8,128]{2,1,0:T(8,128)S(1)} %get-tuple-element.10.tail_pow, ...), custom_call_target="tpu_custom_call" | custom-call | tf_op jit(solution)/shard_map/pallas_call | solution.py:465

commit v7 on v4

--- a/solution.py
+++ b/solution.py
@@ -66,7 +66,7 @@
         pltpu.make_async_copy(w_hbm, w.at[pl.ds(1, nz)], in_sem.at[7]),
         pltpu.make_async_copy(old_hbm, old, in_sem.at[8]),
     ]
-    for load in loads:
+    for load in loads[:4]:
         load.start()
 
     barrier = pltpu.get_barrier_semaphore()
@@ -76,6 +76,9 @@
         )
     for j in (north, south):
         pl.semaphore_signal(barrier, inc=1, device_id={"gy": j}, device_id_type=MESH)
+
+    for load in loads[4:]:
+        load.start()
 
     loads[0].wait()
     loads[1].wait()
@@ -105,22 +108,6 @@
         th = theta[pl.ds(k, 1), :]
         head_pow[k] = jnp.exp(-th * row.astype(F32))
         tail_pow[k] = jnp.exp(-th * (7 - row).astype(F32))
-        level_scale = scale[pl.ds(k, 1), :]
-        near = level_scale * jnp.exp(-th * jnp.abs(row - lane).astype(F32))
-        wrap = level_scale * jnp.exp(-th * (row - lane + m).astype(F32))
-        for b in range(0, blocks, 2):
-            full = jnp.concatenate(
-                [
-                    pltpu.roll(jnp.where(lane < m - 8 * c, near, wrap), 8 * c, 1)
-                    if c
-                    else near
-                    for c in (b, b + 1)
-                ],
-                axis=0,
-            )
-            high = full.astype(BF16)
-            green[k, 8 * b:8 * b + 16, 0:m] = high
-            green[k, 8 * b:8 * b + 16, m:2 * m] = (full - high.astype(F32)).astype(BF16)
         return carry
 
     each_level(0, nz, 4, make_tables, 0)
@@ -221,7 +208,7 @@
         eights[1, k] = head_pow[k] * high_sum
         return carry
 
-    each_level(0, nz, 2, inner, 0)
+    each_level(0, nz, 4, inner, 0)
 
     lane1 = lanes_of((1, m))
     th_lane = jnp.zeros((1, m), F32)
@@ -267,15 +254,40 @@
     moment[0] = sums_low + NEW_TERM_COEF * (q_end * low + top) + spread(weight_g)
     moment[1] = sums_high + NEW_TERM_COEF * (low + q_end * top) + spread(weight_f)
 
-    sends = []
-    for s in range(1, nx):
-        copy = pltpu.make_async_remote_copy(
+    sends = [
+        pltpu.make_async_remote_copy(
             src_ref=moment, dst_ref=moment_got.at[s - 1],
             send_sem=moment_send.at[s - 1], recv_sem=moment_recv.at[s - 1],
             device_id={"gx": lax.rem(gx + s, nx)}, device_id_type=MESH,
         )
+        for s in sorted(range(1, nx), key=lambda s: abs(2 * s - nx))
+    ]
+    for copy in sends:
         copy.start()
-        sends.append(copy)
+
+    def local_inverse(k, carry):
+        row8 = rows_of((8, m))
+        lane8 = lanes_of((8, m))
+        th = theta[pl.ds(k, 1), :]
+        level_scale = scale[pl.ds(k, 1), :]
+        near = level_scale * jnp.exp(-th * jnp.abs(row8 - lane8).astype(F32))
+        wrap = level_scale * jnp.exp(-th * (row8 - lane8 + m).astype(F32))
+        for b0 in range(0, blocks, 2):
+            full = jnp.concatenate(
+                [
+                    pltpu.roll(jnp.where(lane8 < m - 8 * c, near, wrap), 8 * c, 1)
+                    if c
+                    else near
+                    for c in (b0, b0 + 1)
+                ],
+                axis=0,
+            )
+            high = full.astype(BF16)
+            green[k, 8 * b0:8 * b0 + 16, 0:m] = high
+            green[k, 8 * b0:8 * b0 + 16, m:2 * m] = (full - high.astype(F32)).astype(BF16)
+        return carry
+
+    each_level(0, nz, 4, local_inverse, 0)
 
     def local_solve(k, carry):
         lane = lanes_of((q_rows, m))

time: 17.1 us -> 17.9 us (1.047)
  Pallas kernels: 16.3 us -> 17.2 us
    pallas_call x1, Pallas kernels: 14.9 us -> 15.8 us  [on_device(): pl.pallas_call(functools.partial(kernel, nx, ny, nz, m), out_shape=carrie...]
where the time goes in v7:
time: 17.9 us; the launch traced here: 17.8 us
  Pallas kernels  17.2 us (96%)
  between operations  0.64 us (4%)
    pallas_call x1, Pallas kernels, on_device(): pl.pallas_call(functools.partial(kernel, nx, ny, nz, m), out_shape=carrie...  15.8 us
    pallas_call x1, Pallas kernels, on_device(): pl.pallas_call(functools.partial(finish_kernel, nz, m), out_shape=(block,...  1.35 us

profile of v7, /device:TPU:0, one launch (start us, length us, event | category | flops | bytes accessed | tf_op | source)
XLA Modules:
  0.0 17.8 jit_solution(17750582372430053169)
XLA Ops:
  0.6 15.8 %shard_map.86 = (f32[16,128,128]{2,1,0:T(8,128)S(1)}, f32[16,128,128]{2,1,0:T(8,128)S(1)}, f32[16,8,128]{2,1,0:T(8,128)S(1)}, f32[16,8,128]{2,1,0:T(8,128)S(1)}, f32[2,16,16,128]{3,2,1,0:T(8,128)S(1)}) custom-call(f32[16,128,128]{2,1,0:T(8,128)} %t_hbm.1, f32[2,16,128,128]{3,2,1,0:T(8,128)} %uv_hbm.1, f32[16,128,128]{2,1,0:T(8,128)} %w_hbm.1, ...), custom_call_target="tpu_custom_call" | custom-call | flops 268435456 | bytes 8388608 | tf_op jit(solution)/shard_map/pallas_call | solution.py:396
  16.4 1.4 %shard_map.87 = (f32[16,128,128]{2,1,0:T(8,128)}, f32[16,128,128]{2,1,0:T(8,128)}) custom-call(f32[16,128,128]{2,1,0:T(8,128)S(1)} %get-tuple-element.7.part_ref, f32[16,128,128]{2,1,0:T(8,128)S(1)} %get-tuple-element.8.cur_ref, f32[16,8,128]{2,1,0:T(8,128)S(1)} %get-tuple-element.9.head_pow, f32[16,8,128]{2,1,0:T(8,128)S(1)} %get-tuple-element.10.tail_pow, ...), custom_call_target="tpu_custom_call" | custom-call | tf_op jit(solution)/shard_map/pallas_call | solution.py:442

commit v8 on v7

--- a/solution.py
+++ b/solution.py
@@ -254,16 +254,21 @@
     moment[0] = sums_low + NEW_TERM_COEF * (q_end * low + top) + spread(weight_g)
     moment[1] = sums_high + NEW_TERM_COEF * (low + q_end * top) + spread(weight_f)
 
-    sends = [
-        pltpu.make_async_remote_copy(
-            src_ref=moment, dst_ref=moment_got.at[s - 1],
-            send_sem=moment_send.at[s - 1], recv_sem=moment_recv.at[s - 1],
-            device_id={"gx": lax.rem(gx + s, nx)}, device_id_type=MESH,
+    sends = []
+    upper = lax.div(gx, nx // 2)
+    from_end = gx + upper * (nx - 1 - 2 * gx)
+    for j in range(nx - 1):
+        target = nx - 1 - j
+        there = target - lax.div(from_end - target + nx, nx)
+        there = there + upper * (nx - 1 - 2 * there)
+        slot = lax.rem(there - gx + nx, nx) - 1
+        copy = pltpu.make_async_remote_copy(
+            src_ref=moment, dst_ref=moment_got.at[slot],
+            send_sem=moment_send.at[j], recv_sem=moment_recv.at[slot],
+            device_id={"gx": there}, device_id_type=MESH,
         )
-        for s in sorted(range(1, nx), key=lambda s: abs(2 * s - nx))
-    ]
-    for copy in sends:
         copy.start()
+        sends.append(copy)
 
     def local_inverse(k, carry):
         row8 = rows_of((8, m))
@@ -324,8 +329,12 @@
     from_low = powers[nx - 1] * moment[0]
     from_high = powers[nx - 1] * moment[1]
 
-    for copy in sends:
-        copy.wait_recv()
+    for s in range(1, nx):
+        pltpu.make_async_remote_copy(
+            src_ref=moment, dst_ref=moment_got.at[s - 1],
+            send_sem=moment_send.at[s - 1], recv_sem=moment_recv.at[s - 1],
+            device_id={"gx": lax.rem(gx + s, nx)}, device_id_type=MESH,
+        ).wait_recv()
     for s in range(1, nx):
         from_low = from_low + powers[s - 1] * moment_got[s - 1, 0]
         from_high = from_high + powers[nx - s - 1] * moment_got[s - 1, 1]

time: 17.9 us -> 17.1 us (0.955)
  Pallas kernels: 17.2 us -> 16.3 us
    pallas_call x1, Pallas kernels: 15.8 us -> 14.9 us  [on_device(): pl.pallas_call(functools.partial(kernel, nx, ny, nz, m), out_shape=carrie...]
where the time goes in v8:
time: 17.1 us; the launch traced here: 16.9 us
  Pallas kernels  16.3 us (95%)
  between operations  0.64 us (4%)
    pallas_call x1, Pallas kernels, on_device(): pl.pallas_call(functools.partial(kernel, nx, ny, nz, m), out_shape=carrie...  14.9 us
    pallas_call x1, Pallas kernels, on_device(): pl.pallas_call(functools.partial(finish_kernel, nz, m), out_shape=(block,...  1.35 us

profile of v8, /device:TPU:0, one launch (start us, length us, event | category | flops | bytes accessed | tf_op | source)
XLA Modules:
  0.0 16.9 jit_solution(13270551752521564452)
XLA Ops:
  0.6 14.9 %shard_map.86 = (f32[16,128,128]{2,1,0:T(8,128)S(1)}, f32[16,128,128]{2,1,0:T(8,128)S(1)}, f32[16,8,128]{2,1,0:T(8,128)S(1)}, f32[16,8,128]{2,1,0:T(8,128)S(1)}, f32[2,16,16,128]{3,2,1,0:T(8,128)S(1)}) custom-call(f32[16,128,128]{2,1,0:T(8,128)} %t_hbm.1, f32[2,16,128,128]{3,2,1,0:T(8,128)} %uv_hbm.1, f32[16,128,128]{2,1,0:T(8,128)} %w_hbm.1, ...), custom_call_target="tpu_custom_call" | custom-call | flops 268435456 | bytes 8388608 | tf_op jit(solution)/shard_map/pallas_call | solution.py:405
  15.6 1.4 %shard_map.87 = (f32[16,128,128]{2,1,0:T(8,128)}, f32[16,128,128]{2,1,0:T(8,128)}) custom-call(f32[16,128,128]{2,1,0:T(8,128)S(1)} %get-tuple-element.7.part_ref, f32[16,128,128]{2,1,0:T(8,128)S(1)} %get-tuple-element.8.cur_ref, f32[16,8,128]{2,1,0:T(8,128)S(1)} %get-tuple-element.9.head_pow, f32[16,8,128]{2,1,0:T(8,128)S(1)} %get-tuple-element.10.tail_pow, ...), custom_call_target="tpu_custom_call" | custom-call | tf_op jit(solution)/shard_map/pallas_call | solution.py:451

commit v9 on v8

--- a/solution.py
+++ b/solution.py
@@ -208,7 +208,7 @@
         eights[1, k] = head_pow[k] * high_sum
         return carry
 
-    each_level(0, nz, 4, inner, 0)
+    each_level(0, nz, 2, inner, 0)
 
     lane1 = lanes_of((1, m))
     th_lane = jnp.zeros((1, m), F32)

time: 17.1 us -> 17.1 us (level)
  no operation moved by 1% of the time
where the time goes in v9:
time: 17.1 us; the launch traced here: 16.9 us
  Pallas kernels  16.3 us (95%)
  between operations  0.64 us (4%)
    pallas_call x1, Pallas kernels, on_device(): pl.pallas_call(functools.partial(kernel, nx, ny, nz, m), out_shape=carrie...  14.9 us
    pallas_call x1, Pallas kernels, on_device(): pl.pallas_call(functools.partial(finish_kernel, nz, m), out_shape=(block,...  1.35 us

profile of v9, /device:TPU:0, one launch (start us, length us, event | category | flops | bytes accessed | tf_op | source)
XLA Modules:
  0.0 16.9 jit_solution(3649440547803032866)
XLA Ops:
  0.6 14.9 %shard_map.86 = (f32[16,128,128]{2,1,0:T(8,128)S(1)}, f32[16,128,128]{2,1,0:T(8,128)S(1)}, f32[16,8,128]{2,1,0:T(8,128)S(1)}, f32[16,8,128]{2,1,0:T(8,128)S(1)}, f32[2,16,16,128]{3,2,1,0:T(8,128)S(1)}) custom-call(f32[16,128,128]{2,1,0:T(8,128)} %t_hbm.1, f32[2,16,128,128]{3,2,1,0:T(8,128)} %uv_hbm.1, f32[16,128,128]{2,1,0:T(8,128)} %w_hbm.1, ...), custom_call_target="tpu_custom_call" | custom-call | flops 268435456 | bytes 8388608 | tf_op jit(solution)/shard_map/pallas_call | solution.py:405
  15.6 1.4 %shard_map.87 = (f32[16,128,128]{2,1,0:T(8,128)}, f32[16,128,128]{2,1,0:T(8,128)}) custom-call(f32[16,128,128]{2,1,0:T(8,128)S(1)} %get-tuple-element.7.part_ref, f32[16,128,128]{2,1,0:T(8,128)S(1)} %get-tuple-element.8.cur_ref, f32[16,8,128]{2,1,0:T(8,128)S(1)} %get-tuple-element.9.head_pow, f32[16,8,128]{2,1,0:T(8,128)S(1)} %get-tuple-element.10.tail_pow, ...), custom_call_target="tpu_custom_call" | custom-call | tf_op jit(solution)/shard_map/pallas_call | solution.py:451
